TPU v7x, 128 devices: a whole 4x4x4 slice. The times are simulated.
128 devices in a mesh: dp: 8 (over z, x_hi), expert: 16 (over y, x_lo, core).
Axes of the slice: x: 4 (x_hi: 2, x_lo: 2; x = x_hi * 2 + x_lo), y: 4, z: 4, core: 2. Of those that a mesh axis runs over, the one named last changes fastest.
Arguments:
- tokens: bfloat16 [16384, 2560], P(('dp', 'expert')), may hold values from -6 to 6
- expert_ids: int32 [16384, 6], P(('dp', 'expert')), may hold values from 0 to 15, all different within a row; in each aligned block of 128 rows (0 to 127, 128 to 255, ...) at most 56 rows name the same one
- gate_q: int32 [16384, 6], P(('dp', 'expert')), may hold values from 8192 to 65535
- cotangent: bfloat16 [16384, 2560], P(('dp', 'expert')), may hold values from -6 to 6
- placement: int32 [16], replicated, may hold values from 0 to 15, as said below
- weights: bfloat16 [16, 2560, 2304], P('expert'), may hold values from -4 to 4
- moment_one: float32 [16, 2560, 2304], P('expert', 'dp'), may hold values from -1 to 1
- moment_two: float32 [16, 2560, 2304], P('expert', 'dp'), may hold values from 0.001 to 0.3
Outputs:
- token_grad: bfloat16 [16384, 2560], P(('dp', 'expert'))
- new_weights: bfloat16 [16, 2560, 2304], P('expert', 'dp')
- new_moment_one: float32 [16, 2560, 2304], P('expert', 'dp')
- new_moment_two: float32 [16, 2560, 2304], P('expert', 'dp')
Inputs may be any that keep to these rules, and one draw needn't show every extreme that they name: `expert_ids`: in each aligned block of 128 rows (the tokens of one device) no expert is named by more than 56 (token, choice) pairs; some expert is named by exactly 56 in some blocks. placement[e] is e or (e + 8) modulo 16; if e goes to f then f goes to e; in every draw some experts move and some stay.
All inputs are finite; a program needn't handle non-finite values.
Results may differ from a plain program's by a relative error of at most 0.024.
Values may be sent and summed in bfloat16 or wider, within the bound.
A program may use at most 192 MiB of HBM per device.

v0:
```python
import jax
import jax.numpy as jnp
from jax import lax
from jax.sharding import PartitionSpec as P

beta_one = 0.9
beta_two = 0.95
learn_rate = 0.02
decay_rate = 0.1
adam_eps = 1e-08
adam_step = 20.0


def partner(value, axis, apart):
    mask = 2**apart
    pairs = [(source, source ^ mask) for source in range(lax.axis_size(axis))]
    return lax.ppermute(value, axis, pairs)


def slot_index(choices, expert_count, capacity):
    flat_ids = choices.reshape(-1)
    onehot = (flat_ids[:, None] == jnp.arange(expert_count, dtype=jnp.int32)[None, :]).astype(
        jnp.int32
    )
    earlier = jnp.cumsum(onehot, axis=0) - onehot
    position = jnp.sum(earlier * onehot, axis=1)
    return flat_ids * capacity + position


def fill_slots(rows_in, cot_rows, gate_ints, slots, slot_count, top_k):
    pairs = slots.shape[0]
    owner = (
        jnp.zeros((slot_count,), jnp.int32)
        .at[slots]
        .set(jnp.arange(pairs, dtype=jnp.int32) // top_k + 1)
    )
    live = owner > 0
    source = jnp.maximum(owner - 1, 0)
    gates = (
        jnp.zeros((slot_count,), jnp.float32)
        .at[slots]
        .set(gate_ints.reshape(-1).astype(jnp.float32) / 65536.0)
    )
    inputs = jnp.where(live[:, None], rows_in[source], jnp.zeros((), rows_in.dtype))
    scaled = (gates[:, None] * cot_rows[source].astype(jnp.float32)).astype(jnp.bfloat16)
    return (inputs, scaled)


def adam_update(old_rows, grad, first, second):
    first_new = beta_one * first + (1.0 - beta_one) * grad
    second_new = beta_two * second + (1.0 - beta_two) * grad * grad
    first_hat = first_new / (1.0 - beta_one**adam_step)
    second_hat = second_new / (1.0 - beta_two**adam_step)
    weight_f = old_rows.astype(jnp.float32)
    updated = weight_f - learn_rate * (
        first_hat / (jnp.sqrt(second_hat) + adam_eps) + decay_rate * weight_f
    )
    return (updated.astype(jnp.bfloat16), first_new, second_new)


def shards(tokens, expert_ids, gate_q, cotangent, placement, weights, moment_one, moment_two):
    expert_count = lax.axis_size("expert")
    group_count = lax.axis_size("dp")
    tok_rows, top_k = expert_ids.shape
    model_width = tokens.shape[1]
    capacity = tok_rows * top_k * 7 // (6 * expert_count)
    slot_count = expert_count * capacity
    my_slot = lax.axis_index("expert")
    dp_index = lax.axis_index("dp")
    local_weights = weights[0]
    hidden_units = local_weights.shape[1] // 3
    shard_rows = model_width // group_count
    own_rows = lax.dynamic_slice_in_dim(local_weights, dp_index * shard_rows, shard_rows, 0)
    is_moving = placement[my_slot] != my_slot
    swap_bit = expert_count.bit_length() - 2
    slots = slot_index(expert_ids, expert_count, capacity)
    send_inputs, send_cots = fill_slots(tokens, cotangent, gate_q, slots, slot_count, top_k)
    send_inputs = send_inputs.reshape(expert_count, capacity, model_width)
    send_cots = send_cots.reshape(expert_count, capacity, model_width)
    scale_width = model_width ** (-0.5)
    scale_hidden = hidden_units ** (-0.5)
    in_cols = local_weights[:, : 2 * hidden_units]
    down_cols = local_weights[:, 2 * hidden_units :]
    recv_inputs = lax.all_to_all(
        send_inputs, "expert", split_axis=0, concat_axis=0, tiled=True
    ).reshape(slot_count, model_width)
    pre = jnp.dot(recv_inputs, in_cols, preferred_element_type=jnp.float32) * scale_width
    recv_cots = lax.all_to_all(send_cots, "expert", split_axis=0, concat_axis=0, tiled=True)
    recv_cots = recv_cots.reshape(slot_count, model_width)
    gate_part = pre[:, :hidden_units]
    up_part = pre[:, hidden_units:]
    sig = jax.nn.sigmoid(gate_part)
    act = (gate_part * sig * up_part).astype(jnp.bfloat16)
    d_act = jnp.dot(recv_cots, down_cols, preferred_element_type=jnp.float32) * scale_hidden
    d_gate = d_act * up_part * sig * (1.0 + gate_part * (1.0 - sig))
    d_up = d_act * gate_part * sig
    d_hidden = jnp.concatenate([d_gate, d_up], axis=1).astype(jnp.bfloat16)
    partial_dx = lax.dot_general(
        d_hidden, in_cols, (((1,), (1,)), ((), ())), preferred_element_type=jnp.float32
    )
    partial_dx = (
        (partial_dx * scale_width).astype(jnp.bfloat16).reshape(expert_count, capacity, model_width)
    )
    returned = lax.all_to_all(
        partial_dx, "expert", split_axis=0, concat_axis=0, tiled=True
    ).reshape(slot_count, model_width)
    picked = returned[slots].astype(jnp.float32).reshape(tok_rows, top_k, model_width)
    token_grad = jnp.sum(picked, axis=1).astype(jnp.bfloat16)
    grad_in = (
        lax.dot_general(
            recv_inputs, d_hidden, (((0,), (0,)), ((), ())), preferred_element_type=jnp.float32
        )
        * scale_width
    )
    grad_down = (
        lax.dot_general(
            recv_cots, act, (((0,), (0,)), ((), ())), preferred_element_type=jnp.float32
        )
        * scale_hidden
    )
    grad_rows = lax.psum_scatter(
        jnp.concatenate([grad_in, grad_down], axis=1).astype(jnp.bfloat16),
        "dp",
        scatter_dimension=0,
        tiled=True,
    ).astype(jnp.float32)
    upd_rows, upd_one, upd_two = adam_update(own_rows, grad_rows, moment_one[0], moment_two[0])
    sent_one, sent_two = (
        partner(upd_one.astype(jnp.bfloat16), "expert", swap_bit).astype(upd_one.dtype),
        partner(upd_two.astype(jnp.bfloat16), "expert", swap_bit).astype(upd_two.dtype),
    )
    sent_rows = partner(upd_rows, "expert", swap_bit)
    new_rows = jnp.where(is_moving, sent_rows, upd_rows)
    new_one = jnp.where(is_moving, sent_one, upd_one)
    new_two = jnp.where(is_moving, sent_two, upd_two)
    return (token_grad, new_rows[None], new_one[None], new_two[None])


def solution(mesh):
    placed = (
        P(("dp", "expert"), None),
        P(("dp", "expert"), None),
        P(("dp", "expert"), None),
        P(("dp", "expert"), None),
        P(),
        P("expert", None, None),
        P("expert", "dp", None),
        P("expert", "dp", None),
    )
    return jax.shard_map(
        shards,
        mesh=mesh,
        in_specs=placed,
        out_specs=(
            P(("dp", "expert"), None),
            P("expert", "dp", None),
            P("expert", "dp", None),
            P("expert", "dp", None),
        ),
        check_vma=False,
    )
```

profile of v0, /device:TPU:0, one launch (start us, length us, event | category | flops | bytes accessed | tf_op | source)
XLA Modules:
  0.0 522.7 jit_solution(17970681915049175705)
XLA Ops:
  14.9 5.4 %gather_fusion.1 = bf16[896,2560]{1,0:T(8,128)(2,1)} fusion(bf16[128,2560]{1,0:T(8,128)(2,1)S(1)} %copy-done, s32[1024]{0:T(1024)S(1)} %pad_clamp_fusion.1), kind=kCustom, calls=%fused_computation.1 | custom fusion | bytes 9178624 | tf_op jit(solution)/shard_map/gather | solution.py:44
  20.3 4.7 broadcast_select_fusion
  25.0 5.8 %all-to-all-start.1 = ((bf16[16,56,2560]{2,1,0:T(8,128)(2,1)}), bf16[16,56,2560]{2,1,0:T(8,128)(2,1)}, u32[]{:S(2)}, u32[]{:S(2)}) async-start(bf16[16,56,2560]{2,1,0:T(8,128)(2,1)} %broadcast_select_fusion), calls=%async_computation.1 | async-start | bytes 9175040 | tf_op jit(solution)/shard_map/all_to_all | solution.py:84
  30.8 5.3 %gather_fusion = bf16[896,2560]{1,0:T(8,128)(2,1)} fusion(bf16[128,2560]{1,0:T(8,128)(2,1)S(1)} %copy-done.2, s32[1024]{0:T(1024)S(1)} %pad_clamp_fusion.1), kind=kCustom, calls=%fused_computation | custom fusion | bytes 9178624 | tf_op jit(solution)/shard_map/gather | solution.py:45
  39.9 5.2 fusion
  45.0 40.4 %all-to-all-done.1 = bf16[16,56,2560]{2,1,0:T(8,128)(2,1)} async-done(((bf16[16,56,2560]{2,1,0:T(8,128)(2,1)}), bf16[16,56,2560]{2,1,0:T(8,128)(2,1)}, u32[]{:S(2)}, u32[]{:S(2)}) %all-to-all-start.1) | async-done | bytes 4587552 | tf_op jit(solution)/shard_map/all_to_all | solution.py:84
  85.4 4.6 all-to-all-start
  90.5 13.7 %fusion.7 = f32[896,1536]{0,1:T(8,128)} fusion(bf16[896,2560]{1,0:T(8,128)(2,1)} %bitcast.5, bf16[2560,2304]{1,0:T(8,128)(2,1)} %bitcast.62), kind=kOutput, calls=%fused_computation.17 | convolution fusion | flops 7047806976 | bytes 17956864 | tf_op jit(solution)/shard_map/dot_general | solution.py:87
  104.2 40.4 %all-to-all-done = bf16[16,56,2560]{2,1,0:T(8,128)(2,1)} async-done(((bf16[16,56,2560]{2,1,0:T(8,128)(2,1)}), bf16[16,56,2560]{2,1,0:T(8,128)(2,1)}, u32[]{:S(2)}, u32[]{:S(2)}) %all-to-all-start) | async-done | bytes 4587552 | tf_op jit(solution)/shard_map/all_to_all | solution.py:88
  144.6 10.5 %multiply_convert_fusion.5 = (bf16[896,768]{0,1:T(8,128)(2,1)S(1)}, bf16[896,768]{0,1:T(8,128)(2,1)S(1)}) fusion(f32[896,1536]{0,1:T(8,128)} %fusion.7, bf16[896,2560]{1,0:T(8,128)(2,1)} %bitcast.2, bf16[2560,2304]{1,0:T(8,128)(2,1)} %bitcast.63), kind=kOutput, calls=%fused_computation.33 | convolution fusion | flops 3532849152 | bytes 16777216 | tf_op jit(solution)/shard_map/dot_general | solution.py:94
  155.1 7.8 %multiply_convert_fusion.2 = bf16[2560,768]{0,1:T(8,128)(2,1)S(1)} fusion(bf16[896,2560]{1,0:T(8,128)(2,1)} %bitcast.2, f32[896,1536]{0,1:T(8,128)S(1)} %copy-done.6), kind=kOutput, calls=%fused_computation.10 | convolution fusion | flops 3531276288 | bytes 14024704 | tf_op jit(solution)/shard_map/dot_general | solution.py:116
  163.0 12.3 %multiply_convert_fusion = bf16[2560,1536]{0,1:T(8,128)(2,1)S(1)} fusion(bf16[896,2560]{1,0:T(8,128)(2,1)} %bitcast.5, bf16[896,768]{0,1:T(8,128)(2,1)S(1)} %get-tuple-element.17, bf16[896,768]{0,1:T(8,128)(2,1)S(1)} %get-tuple-element.16), kind=kOutput, calls=%fused_computation.5 | convolution fusion | flops 7059800064 | bytes 15204352 | tf_op jit(solution)/shard_map/dot_general | solution.py:110
  175.3 12.3 %pad_maximum_fusion = bf16[2560,2304]{0,1:T(8,128)(2,1)} fusion(bf16[2560,768]{0,1:T(8,128)(2,1)S(1)} %multiply_convert_fusion.2, bf16[2560,1536]{0,1:T(8,128)(2,1)S(1)} %multiply_convert_fusion), kind=kLoop, calls=%fused_computation.6 | loop fusion | flops 23592960 | bytes 23592960 | tf_op jit(solution)/shard_map/concatenate | solution.py:122
  187.6 15.0 %copy.50 = bf16[2560,2304]{1,0:T(8,128)(2,1)} copy(bf16[2560,2304]{0,1:T(8,128)(2,1)} %pad_maximum_fusion) | data formatting | bytes 23592960
  202.6 4.9 copy.39
  207.5 139.7 %reduce-scatter.4.cloned.1.call-done = bf16[320,2304]{1,0:T(8,128)(2,1)} async-done(((bf16[2560,2304]{1,0:T(8,128)(2,1)}), bf16[320,2304]{1,0:T(8,128)(2,1)}) %reduce-scatter.4.cloned.1.call-update) | async-done | bytes 1474576
  350.0 3.9 fusion.19
  360.6 12.0 %multiply_convert_fusion.1 = bf16[896,2560]{1,0:T(8,128)(2,1)} fusion(bf16[2560,2304]{1,0:T(8,128)(2,1)} %bitcast.64, bf16[896,768]{0,1:T(8,128)(2,1)} %copy-done.8, bf16[896,768]{0,1:T(8,128)(2,1)} %copy-done.7), kind=kOutput, calls=%fused_computation.9 | convolution fusion | flops 7056523264 | bytes 15204352 | tf_op jit(solution)/shard_map/dot_general | solution.py:98
  372.6 4.9 all-to-all-start.2
  385.0 4.9 copy.38
  389.9 22.1 %collective-permute-done.2 = bf16[320,2304]{1,0:T(8,128)(2,1)} collective-permute-done((bf16[320,2304]{1,0:T(8,128)(2,1)}, bf16[320,2304]{1,0:T(8,128)(2,1)}, u32[]{:S(2)}, u32[]{:S(2)}) %collective-permute-start.2) | collective-permute-done | bytes 1474592 | tf_op jit(solution)/shard_map/ppermute | solution.py:17
  415.6 8.7 %select_bitcast_fusion = (f32[1,320,2304]{1,2,0:T(8,128)}, bf16[320,2304]{0,1:T(8,128)(2,1)}, bf16[320,2304]{0,1:T(8,128)(2,1)}) fusion(bf16[320,2304]{0,1:T(8,128)(2,1)} %copy.45, pred[]{:T(512)S(6)} %ne.20, bf16[320,2304]{0,1:T(8,128)(2,1)S(1)} %copy.51, f32[1,320,2304]{1,2,0:T(8,128)} %copy.39, f32[1,320,2304]{1,2,0:T(8,128)} %copy.38, ...), kind=kLoop, calls=%fused_computation.28 | loop fusion | flops 15482880 | bytes 16220161 | tf_op jit(solution)/shard_map/broadcast_in_dim | solution.py:136
  428.0 4.2 collective-permute-start.1
  435.9 7.0 %all-to-all-done.2 = bf16[16,56,2560]{2,1,0:T(8,128)(2,1)} async-done(((bf16[16,56,2560]{2,1,0:T(8,128)(2,1)}), bf16[16,56,2560]{2,1,0:T(8,128)(2,1)}, u32[]{:S(2)}, u32[]{:S(2)}) %all-to-all-start.2) | async-done | bytes 4587552 | tf_op jit(solution)/shard_map/all_to_all | solution.py:104
  442.9 11.3 %gather_fusion.2 = bf16[768,2560]{1,0:T(8,128)(2,1)} fusion(bf16[896,2560]{1,0:T(8,128)(2,1)} %bitcast.7, s32[1024]{0:T(1024)S(1)} %pad_clamp_fusion), kind=kCustom, calls=%fused_computation.2 | custom fusion | bytes 7867392 | tf_op jit(solution)/shard_map/gather | solution.py:107
  454.2 7.1 %gather.17 = bf16[128,6,2560]{2,1,0:T(8,128)(2,1)} reshape(bf16[768,2560]{1,0:T(8,128)(2,1)} %gather_fusion.2) | data formatting | bytes 7864320 | tf_op jit(solution)/shard_map/gather | solution.py:107
  461.3 6.5 %reduce_sum.25 = bf16[128,2560]{1,0:T(8,128)(2,1)} reduce(bf16[128,6,2560]{2,1,0:T(8,128)(2,1)} %gather.17, bf16[]{:T(256)} %constant.35.clone.1), dimensions={1}, to_apply=%region_5.6 | reduce | flops 1638400 | bytes 4587522 | tf_op jit(solution)/shard_map/reduce_sum | solution.py:108
  467.9 4.9 copy.48
  479.1 5.0 select_bitcast_fusion.1
  484.1 5.0 copy.47
  489.1 16.1 %collective-permute-done = bf16[320,2304]{1,0:T(8,128)(2,1)} collective-permute-done((bf16[320,2304]{1,0:T(8,128)(2,1)}, bf16[320,2304]{1,0:T(8,128)(2,1)}, u32[]{:S(2)}, u32[]{:S(2)}) %collective-permute-start) | collective-permute-done | bytes 1474592 | tf_op jit(solution)/shard_map/ppermute | solution.py:17
  505.2 3.8 copy.41
  (58 shorter events, 52.3 us)
Async XLA Ops:
  7.2 7.8 %copy-start = (bf16[128,2560]{1,0:T(8,128)(2,1)S(1)}, bf16[128,2560]{1,0:T(8,128)(2,1)}, u32[]{:S(2)}) copy-start(bf16[128,2560]{1,0:T(8,128)(2,1)} %param.8) | copy-start | bytes 1966084
  25.0 5.8 %copy-start.2 = (bf16[128,2560]{1,0:T(8,128)(2,1)S(1)}, bf16[128,2560]{1,0:T(8,128)(2,1)}, u32[]{:S(2)}) copy-start(bf16[128,2560]{1,0:T(8,128)(2,1)} %param.11) | copy-start | bytes 1966084
  25.0 60.4 %all-to-all-start.1 = ((bf16[16,56,2560]{2,1,0:T(8,128)(2,1)}), bf16[16,56,2560]{2,1,0:T(8,128)(2,1)}, u32[]{:S(2)}, u32[]{:S(2)}) async-start(bf16[16,56,2560]{2,1,0:T(8,128)(2,1)} %broadcast_select_fusion), calls=%async_computation.1 | async-start | bytes 9175040 | tf_op jit(solution)/shard_map/all_to_all | solution.py:84
  30.8 5.3 %copy-start.4 = (s32[128,6]{0,1:T(8,128)S(1)}, s32[128,6]{0,1:T(8,128)}, u32[]{:S(2)}) copy-start(s32[128,6]{0,1:T(8,128)} %param.10) | copy-start | bytes 9220
  85.4 59.1 %all-to-all-start = ((bf16[16,56,2560]{2,1,0:T(8,128)(2,1)}), bf16[16,56,2560]{2,1,0:T(8,128)(2,1)}, u32[]{:S(2)}, u32[]{:S(2)}) async-start(bf16[16,56,2560]{2,1,0:T(8,128)(2,1)} %fusion), calls=%async_computation | async-start | bytes 9175040 | tf_op jit(solution)/shard_map/all_to_all | solution.py:88
  90.0 257.3 %reduce-scatter.4.cloned.1.call-start = ((), (), s32[]{:S(2)}) async-start(), calls=%async_computation.4 | async-start | bytes 13271040
  144.6 10.5 %copy-start.6 = (f32[896,1536]{0,1:T(8,128)S(1)}, f32[896,1536]{0,1:T(8,128)}, u32[]{:S(2)}) copy-start(f32[896,1536]{0,1:T(8,128)} %fusion.7) | copy-start | bytes 16515076
  155.1 7.9 %copy-start.7 = (bf16[896,768]{0,1:T(8,128)(2,1)}, bf16[896,768]{0,1:T(8,128)(2,1)S(1)}, u32[]{:S(2)}) copy-start(bf16[896,768]{0,1:T(8,128)(2,1)S(1)} %get-tuple-element.16) | copy-start | bytes 4128772
  155.1 7.9 %copy-start.8 = (bf16[896,768]{0,1:T(8,128)(2,1)}, bf16[896,768]{0,1:T(8,128)(2,1)S(1)}, u32[]{:S(2)}) copy-start(bf16[896,768]{0,1:T(8,128)(2,1)S(1)} %get-tuple-element.17) | copy-start | bytes 4128772
  357.6 54.4 %collective-permute-start.2 = (bf16[320,2304]{1,0:T(8,128)(2,1)}, bf16[320,2304]{1,0:T(8,128)(2,1)}, u32[]{:S(2)}, u32[]{:S(2)}) collective-permute-start(bf16[320,2304]{1,0:T(8,128)(2,1)} %copy.44), channel_id=1, source_target_pairs={{0,8},{1,9},{2,10},{3,11},{4,12},{5,13},{6,14},{7,15},{8,0},{9,1},... | collective-permute-start | bytes 4423688 | tf_op jit(solution)/shard_map/ppermute | solution.py:17
  372.6 4.9 copy-start.5
  372.6 70.3 %all-to-all-start.2 = ((bf16[16,56,2560]{2,1,0:T(8,128)(2,1)}), bf16[16,56,2560]{2,1,0:T(8,128)(2,1)}, u32[]{:S(2)}, u32[]{:S(2)}) async-start(bf16[16,56,2560]{2,1,0:T(8,128)(2,1)} %bitcast.61), calls=%async_computation.2 | async-start | bytes 9175040 | tf_op jit(solution)/shard_map/all_to_all | solution.py:104
  428.0 47.4 %collective-permute-start.1 = (bf16[320,2304]{1,0:T(8,128)(2,1)}, bf16[320,2304]{1,0:T(8,128)(2,1)}, u32[]{:S(2)}, u32[]{:S(2)}) collective-permute-start(bf16[320,2304]{1,0:T(8,128)(2,1)} %copy.42), channel_id=1, source_target_pairs={{0,8},{1,9},{2,10},{3,11},{4,12},{5,13},{6,14},{7,15},{8,0},{9,1},... | collective-permute-start | bytes 4423688 | tf_op jit(solution)/shard_map/ppermute | solution.py:17
  435.9 69.3 %collective-permute-start = (bf16[320,2304]{1,0:T(8,128)(2,1)}, bf16[320,2304]{1,0:T(8,128)(2,1)}, u32[]{:S(2)}, u32[]{:S(2)}) collective-permute-start(bf16[320,2304]{1,0:T(8,128)(2,1)} %copy.40), channel_id=1, source_target_pairs={{0,8},{1,9},{2,10},{3,11},{4,12},{5,13},{6,14},{7,15},{8,0},{9,1},... | collective-permute-start | bytes 4423688 | tf_op jit(solution)/shard_map/ppermute | solution.py:17
  484.1 24.9 %copy-start.3 = (bf16[320,2304]{0,1:T(8,128)(2,1)S(1)}, bf16[320,2304]{0,1:T(8,128)(2,1)}, u32[]{:S(2)}) copy-start(bf16[320,2304]{0,1:T(8,128)(2,1)} %get-tuple-element.19) | copy-start | bytes 4423684
  505.2 10.4 %copy-start.1 = (bf16[128,2560]{1,0:T(8,128)(2,1)S(1)}, bf16[128,2560]{1,0:T(8,128)(2,1)}, u32[]{:S(2)}) copy-start(bf16[128,2560]{1,0:T(8,128)(2,1)} %param.8) | copy-start | bytes 1966084
Sparse Core Ops, SparseCore 0:
  202.7 144.4 reduce-scatter.3
where the time goes:
time: 530 us; the launch traced here: 523 us
  waiting for transfers between devices  268 us (51%)
  local copies, waits for them, and re-layouts  108 us (20%)
  matrix products  56.3 us (11%)
  other arithmetic  51.7 us (10%)
  starting transfers between devices  22.9 us (4%)
  between operations  15.2 us (3%)
    unnamed x2, waiting for transfers between devices  140 us
    unnamed x27, local copies, waits for them, and re-layouts  45.7 us
    ppermute x3, waiting for transfers between devices, partner(): return lax.ppermute(value, axis, pairs)  40.8 us
    all_to_all x1, waiting for transfers between devices, shards(): lax.all_to_all(send_cots, 'expert', split_axis=0, concat_axis=0, tiled=True)  40.4 us
    all_to_all x1, waiting for transfers between devices, shards(): lax.all_to_all(send_inputs, 'expert', split_axis=0, concat_axis=0, tiled=...  40.4 us
    gather x2, local copies, waits for them, and re-layouts, shards(): returned[slots].astype(jnp.float32).reshape(tok_rows, top_k, model_width)  18.5 us
    broadcast_in_dim x3, other arithmetic, shards(): return (token_grad, new_rows[None], new_one[None], new_two[None])  16.6 us
    dot_general x1, matrix products, shards(): jnp.dot(recv_inputs, in_cols, preferred_element_type=jnp.float32)  13.7 us
  transfers between devices with their start and end apart: 7, of which 7 were waited for; matrix products, arithmetic and copies ran while one was open for 23% of the time, Pallas kernels for 0%

commit v1 on v0

v1 whole, which is shorter than its diff:
```python
import functools

import jax
import jax.numpy as jnp
from jax import lax
from jax.experimental import pallas as pl
from jax.experimental.pallas import tpu as pltpu
from jax.sharding import PartitionSpec as P

beta_one = 0.9
beta_two = 0.95
learn_rate = 0.02
decay_rate = 0.1
adam_eps = 1e-08
adam_step = 20.0

MESH = pl.DeviceIdType.MESH
ANY = pl.BlockSpec(memory_space=pl.ANY)
VMEM = pl.BlockSpec(memory_space=pltpu.VMEM)

ORDER = (0, 1, 2, 3, 6, 7, 4, 5)
BATCHES = ((0, 1), (2, 3, 6, 7), (4, 5))


def coords():
    dp = lax.axis_index("dp")
    e = lax.axis_index("expert")
    return dp, e, e // 4, (e // 2) % 2, e % 2


def peer(dy, dl, dc):
    dp, _, y, l, c = coords()
    y2 = (y + dy) % 4 if dy else y
    l2 = 1 - l if dl else l
    c2 = 1 - c if dc else c
    return (dp, y2 * 4 + l2 * 2 + c2)


def dispatch_kernel(
    scales,
    tok,
    cot,
    pack,
    w,
    x_out,
    c_out,
    ha_out,
    p_out,
    gathered,
    ids,
    mrow,
    grow,
    gcol,
    onehot,
    wv,
    stage,
    xc,
    pre,
    ha,
    psend,
    precv,
    send,
    recv,
    local,
    outs,
):
    scale_w, scale_h = scales
    _, me, _, _, _ = coords()
    half, cap = 64, 56
    pair = 2 * cap
    hid = pre.shape[1] // 2
    others = [(dy, dl, dc) for dy in range(4) for dl in range(2) for dc in range(2)][1:]

    barrier = pltpu.get_barrier_semaphore()
    for o in others:
        pl.semaphore_signal(barrier, inc=1, device_id=peer(*o), device_id_type=MESH)
    pl.semaphore_wait(barrier, len(others))

    packs = []
    for n, (dy, dl, dc) in enumerate(others):
        seen = ((4 - dy) % 4) * 2 + dl
        packs.append(
            pltpu.make_async_remote_copy(
                src_ref=pack,
                dst_ref=ids.at[2 * seen + dc],
                send_sem=psend.at[n],
                recv_sem=precv.at[n],
                device_id=peer(dy, dl, dc),
                device_id_type=MESH,
            )
        )
    for d in packs:
        d.start()

    flight = {}

    def go(i, key, src, r, rows, to):
        n = len(flight)
        d = pltpu.make_async_remote_copy(
            src_ref=src,
            dst_ref=gathered.at[i, r, pl.ds(128 * to[2] + rows[0], rows[1] - rows[0])],
            send_sem=send.at[n],
            recv_sem=recv.at[n],
            device_id=peer(*to),
            device_id_type=MESH,
        )
        d.start()
        flight[(i, key)] = d

    UP, DOWN, ACROSS, SIB = (1, 0, 0), (3, 0, 0), (0, 1, 0), (0, 0, 1)
    own = (tok, cot)

    def mine(i, lo, hi):
        return own[i].at[pl.ds(lo, hi - lo)]

    def got(i, r, lo, hi):
        return gathered.at[i, r, pl.ds(lo, hi - lo)]

    def share(i, r, lo, hi):
        go(i, ("S", r, lo), got(i, r, lo, hi), r, (lo, hi), SIB)

    def land(i, key):
        flight[(i, key)].wait_recv()

    def first(i):
        go(i, "A1", mine(i, 0, 64), 1, (0, 64), ACROSS)
        go(i, "A2p0", mine(i, 0, 64), 6, (0, 64), UP)
        go(i, "A2m0", mine(i, 0, 64), 2, (0, 64), DOWN)
        go(i, "B1p", mine(i, 64, 128), 6, (64, 128), UP)
        go(i, "B1m", mine(i, 64, 128), 2, (64, 128), DOWN)
        go(i, "B30", mine(i, 64, 128), 1, (64, 128), ACROSS)
        go(i, ("S", 0, 0), own[i], 0, (0, 128), SIB)

    def second(i):
        land(i, "A1")
        go(i, "A2p1", got(i, 1, 0, 64), 7, (0, 64), UP)
        go(i, "A2m1", got(i, 1, 0, 64), 3, (0, 64), DOWN)
        share(i, 1, 0, 64)
        land(i, "A2p0")
        go(i, "A3p0", got(i, 6, 0, 32), 4, (0, 32), UP)
        share(i, 6, 0, 64)
        land(i, "A2m0")
        go(i, "A3m0", got(i, 2, 32, 64), 4, (32, 64), DOWN)
        share(i, 2, 0, 64)

    def third(i):
        land(i, "B1p")
        go(i, "B33", got(i, 6, 64, 128), 7, (64, 128), ACROSS)
        go(i, "B2p", got(i, 6, 64, 96), 4, (64, 96), UP)
        share(i, 6, 64, 128)
        land(i, "B1m")
        go(i, "B31", got(i, 2, 64, 128), 3, (64, 128), ACROSS)
        go(i, "B2m", got(i, 2, 96, 128), 4, (96, 128), DOWN)
        share(i, 2, 64, 128)
        land(i, "B30")
        share(i, 1, 64, 128)

    def fourth(i):
        land(i, "A2p1")
        go(i, "A3p1", got(i, 7, 0, 32), 5, (0, 32), UP)
        share(i, 7, 0, 64)
        land(i, "A2m1")
        go(i, "A3m1", got(i, 3, 32, 64), 5, (32, 64), DOWN)
        share(i, 3, 0, 64)
        land(i, "B2p")
        land(i, "B2m")
        go(i, "B32", got(i, 4, 64, 128), 5, (64, 128), ACROSS)
        land(i, "A3p0")
        land(i, "A3m0")
        share(i, 4, 0, 64)
        share(i, 4, 64, 128)
        land(i, "B33")
        share(i, 7, 64, 128)
        land(i, "B31")
        share(i, 3, 64, 128)

    def fifth(i):
        land(i, "A3p1")
        land(i, "A3m1")
        share(i, 5, 0, 64)
        land(i, "B32")
        share(i, 5, 64, 128)

    def fetch(i, batch):
        copies = []
        for n, r in enumerate(batch):
            if r == 0:
                land(i, ("S", 0, 0))
                copies.append(pltpu.make_async_copy(own[i], stage.at[n, pl.ds(0, 128)], local.at[n]))
                copies.append(
                    pltpu.make_async_copy(
                        gathered.at[i, 0, pl.ds(128, 128)], stage.at[n, pl.ds(128, 128)], local.at[4]
                    )
                )
            else:
                land(i, ("S", r, 0))
                land(i, ("S", r, 64))
                copies.append(pltpu.make_async_copy(gathered.at[i, r], stage.at[n], local.at[n]))
        for d in copies:
            d.start()
        for d in copies:
            d.wait()

    def pick(i, batch):
        fetch(i, batch)
        for n, r in enumerate(batch):
            at = ORDER.index(r) * pair
            rows = jnp.dot(onehot[r], stage[n], preferred_element_type=jnp.float32)
            if i == 1:
                rows = rows * gcol[pl.ds(at, pair), :]
            xc[i, pl.ds(at, pair), :] = rows.astype(jnp.bfloat16)

    def span(batch):
        return ORDER.index(batch[0]) * pair, len(batch) * pair

    def forward(batch):
        at, size = span(batch)
        wide = 512

        @pl.loop(0, 2 * hid // wide)
        def _(n):
            cols = pl.ds(pl.multiple_of(n * wide, wide), wide)
            pre[pl.ds(at, size), cols] = (
                jnp.dot(xc[0, pl.ds(at, size), :], wv[:, cols], preferred_element_type=jnp.float32)
                * scale_w
            )

    def backward(batch):
        at, size = span(batch)
        wide = 256

        @pl.loop(0, hid // wide)
        def _(n):
            def cols(start):
                return pl.ds(pl.multiple_of(start + n * wide, wide), wide)

            rows = pl.ds(at, size)
            da = (
                jnp.dot(xc[1, rows, :], wv[:, cols(2 * hid)], preferred_element_type=jnp.float32)
                * scale_h
            )
            gate = pre[rows, cols(0)]
            up = pre[rows, cols(hid)]
            sig = jax.nn.sigmoid(gate)
            gs = gate * sig
            ha[rows, cols(0)] = (da * up * sig * (1.0 + gate * (1.0 - sig))).astype(jnp.bfloat16)
            ha[rows, cols(hid)] = (da * gs).astype(jnp.bfloat16)
            ha[rows, cols(2 * hid)] = (gs * up).astype(jnp.bfloat16)

    first(0)
    weights_in = pltpu.make_async_copy(w, wv, local.at[5])
    weights_in.start()
    for d in packs:
        d.wait_recv()
    ids[0] = pack[...]
    for s in range(16):
        chosen = ids[s, 0:8, :] == me
        mrow[s : s + 1, :] = jnp.sum(
            jnp.where(chosen, 1.0, 0.0), axis=0, keepdims=True
        )
        grow[s : s + 1, :] = jnp.sum(
            jnp.where(chosen, ids[s, 8:16, :].astype(jnp.float32), 0.0), axis=0, keepdims=True
        ) * (1.0 / 65536.0)
    second(0)
    before = (
        lax.broadcasted_iota(jnp.int32, (128, 128), 0) < lax.broadcasted_iota(jnp.int32, (128, 128), 1)
    ).astype(jnp.bfloat16)
    position = jnp.dot(mrow[...].astype(jnp.bfloat16), before, preferred_element_type=jnp.float32)
    mrow[...] = jnp.where(mrow[...] > 0.5, position, -1000.0)
    slot = lax.broadcasted_iota(jnp.int32, (pair, 256), 0).astype(jnp.float32)
    for r in range(8):
        place = jnp.concatenate([mrow[2 * r : 2 * r + 1, :], mrow[2 * r + 1 : 2 * r + 2, :] + cap], axis=1)
        gate_row = jnp.concatenate([grow[2 * r : 2 * r + 1, :], grow[2 * r + 1 : 2 * r + 2, :]], axis=1)
        hit = jnp.where(slot == place, 1.0, 0.0)
        onehot[r] = hit.astype(jnp.bfloat16)
        gcol[pl.ds(ORDER.index(r) * pair, pair), :] = jnp.sum(hit * gate_row, axis=1, keepdims=True)
    third(0)
    first(1)
    fourth(0)
    pick(0, BATCHES[0])
    second(1)
    weights_in.wait()
    forward(BATCHES[0])
    fifth(0)
    third(1)
    pick(0, BATCHES[1])
    forward(BATCHES[1])
    fourth(1)
    pick(0, BATCHES[2])
    forward(BATCHES[2])
    done = [pltpu.make_async_copy(xc.at[0], x_out, outs.at[0]), pltpu.make_async_copy(onehot, p_out, outs.at[1])]
    for d in done:
        d.start()
    pick(1, BATCHES[0])
    backward(BATCHES[0])
    fifth(1)
    pick(1, BATCHES[1])
    backward(BATCHES[1])
    pick(1, BATCHES[2])
    backward(BATCHES[2])
    last = [pltpu.make_async_copy(xc.at[1], c_out, outs.at[2]), pltpu.make_async_copy(ha, ha_out, outs.at[3])]
    for d in last:
        d.start()
    for d in packs:
        d.wait_send()
    for d in flight.values():
        d.wait_send()
    for d in done + last:
        d.wait()


def dispatch(tokens, cotangent, pack, weights, scales):
    width = tokens.shape[1]
    total = weights.shape[1]
    hid = total // 3
    slots = 896
    bf, f32 = jnp.bfloat16, jnp.float32
    sems = pltpu.SemaphoreType.DMA
    return pl.pallas_call(
        functools.partial(dispatch_kernel, scales),
        name="dispatch",
        out_shape=(
            jax.ShapeDtypeStruct((slots, width), bf),
            jax.ShapeDtypeStruct((slots, width), bf),
            jax.ShapeDtypeStruct((slots, total), bf),
            jax.ShapeDtypeStruct((8, 112, 256), bf),
            jax.ShapeDtypeStruct((2, 8, 256, width), bf),
        ),
        in_specs=[ANY, ANY, VMEM, ANY],
        out_specs=(ANY,) * 5,
        scratch_shapes=[
            pltpu.VMEM((16, 16, 128), jnp.int32),
            pltpu.VMEM((16, 128), f32),
            pltpu.VMEM((16, 128), f32),
            pltpu.VMEM((slots, 1), f32),
            pltpu.VMEM((8, 112, 256), bf),
            pltpu.VMEM((width, total), bf),
            pltpu.VMEM((4, 256, width), bf),
            pltpu.VMEM((2, slots, width), bf),
            pltpu.VMEM((slots, 2 * hid), f32),
            pltpu.VMEM((slots, total), bf),
            sems((15,)),
            sems((15,)),
            sems((64,)),
            sems((64,)),
            sems((6,)),
            sems((4,)),
        ],
        compiler_params=pltpu.CompilerParams(
            collective_id=1, has_side_effects=True, vmem_limit_bytes=60 * 2**20
        ),
    )(tokens, cotangent, pack, weights)


def reduce_kernel(
    scales,
    x_in,
    c_in,
    ha_in,
    p_in,
    w,
    m_in,
    v_in,
    tok_grad,
    m_out,
    v_out,
    w_got,
    m_got,
    v_got,
    xt,
    ha,
    onehot,
    raw,
    g_send,
    r1,
    r2,
    x_send,
    x_recv,
    m_stage,
    v_stage,
    m_new,
    v_new,
    m_send,
    v_send,
    w_stage,
    pick,
    s_send,
    s_own,
    s_recv,
    l_recv,
    l_own,
    l_send,
    y1,
    y2,
    y_send,
    t_out,
    far_send,
    far_recv,
    load,
    z_send,
    r1_sem,
    r2_sem,
    xs_sem,
    xr_sem,
    state,
    new_sem,
    ms_sem,
    mr_sem,
    ss_sem,
    sr_sem,
    ls_sem,
    lr_sem,
    ys_sem,
    yr_sem,
    t_sem,
):
    scale_w, scale_h = scales
    dp, e, y, l, c = coords()
    z, h = dp // 2, dp % 2
    bf, f32 = jnp.bfloat16, jnp.float32
    up_z = (((z + 1) % 4) * 2 + h, e)
    down_z = (((z + 3) % 4) * 2 + h, e)
    other_h = (z * 2 + 1 - h, e)
    far = peer(2, 0, 0)
    sib = peer(0, 0, 1)
    across = peer(0, 1, 0)
    up_y = peer(1, 0, 0)
    down_y = peer(3, 0, 0)

    n_chunk, n_col = 9, 5
    cw = 256
    dw = 512
    quarter, eighth = 640, 320
    hid2 = 1536
    pair = 112

    barrier = pltpu.get_barrier_semaphore()
    greet = [up_z, down_z, other_h, far, sib, across, up_y, down_y]
    for d in greet:
        pl.semaphore_signal(barrier, inc=1, device_id=d, device_id_type=MESH)
    loads = [
        pltpu.make_async_copy(ha_in, ha, load.at[0]),
        pltpu.make_async_copy(p_in, onehot, load.at[1]),
    ]
    for d in loads:
        d.start()

    def raw_copy(i, q, slot):
        src = c_in if i else x_in
        start = pl.multiple_of(((z + q) % 4) * quarter, quarter)
        return pltpu.make_async_copy(src.at[:, pl.ds(start, quarter)], raw.at[slot], load.at[2 + slot])

    raw_copy(0, 2, 0).start()
    raw_copy(0, 1, 1).start()
    pl.semaphore_wait(barrier, len(greet))

    def remote(src, dst, ssem, rsem, to):
        return pltpu.make_async_remote_copy(
            src_ref=src, dst_ref=dst, send_sem=ssem, recv_sem=rsem, device_id=to, device_id_type=MESH
        )

    own_rows = pl.ds(pl.multiple_of(dp * eighth, eighth), eighth)
    far_w = remote(w.at[own_rows], w_got, far_send, far_recv, far)

    def turn(i, q, slot):
        raw_copy(i, q, slot).wait()
        for j in range(quarter // 128):
            xt[i, q, pl.ds(j * 128, 128), :] = raw[slot, :, pl.ds(j * 128, 128)].T

    turn(0, 2, 0)
    raw_copy(0, 3, 0).start()
    turn(0, 1, 1)
    raw_copy(0, 0, 1).start()
    loads[0].wait()
    turn(0, 3, 0)
    turn(0, 0, 1)
    loads[1].wait()
    raw_copy(1, 2, 0).start()
    raw_copy(1, 1, 1).start()
    turn(1, 2, 0)
    raw_copy(1, 3, 0).start()
    turn(1, 1, 1)
    raw_copy(1, 0, 1).start()
    turn(1, 3, 0)
    turn(1, 0, 1)

    def cols(k):
        return pl.ds(pl.multiple_of(k * cw, cw), cw)

    def product(k, q):
        scale = jnp.where(k < 6, scale_w, scale_h).astype(f32)
        return (
            jnp.dot(xt[k // 6, q], ha[:, cols(k)], preferred_element_type=f32) * scale
        )

    lo, hi = pl.ds(0, eighth), pl.ds(eighth, eighth)

    def z_copy(k, n):
        s = k % 3
        src = (
            g_send.at[s, 1, lo],
            g_send.at[s, 1, hi],
            g_send.at[s, 0, hi],
            g_send.at[s, 2, lo],
            g_send.at[s, 0, lo],
            g_send.at[s, 2, hi],
        )[n]
        dst = (
            r1.at[k, 0],
            r1.at[k, 1],
            r2.at[k, 0, hi],
            r2.at[k, 1, lo],
            r2.at[k, 0, lo],
            r2.at[k, 1, hi],
        )[n]
        rsem = (r1_sem.at[k, 0], r1_sem.at[k, 1], r2_sem.at[k, 0], r2_sem.at[k, 1], r2_sem.at[k, 2], r2_sem.at[k, 3])[n]
        return remote(src, dst, z_send.at[s, n], rsem, up_z if n % 2 == 0 else down_z)

    def h_copy(k):
        return remote(x_send.at[k % 2], x_recv.at[k], xs_sem.at[k % 2], xr_sem.at[k], other_h)

    def m_copy(k, n):
        src = (m_send, v_send)[n].at[k % 2]
        dst = (m_got, v_got)[n].at[:, cols(k)]
        return remote(src, dst, ms_sem.at[k % 2, n], mr_sem.at[k, n], far)

    def state_in(k, n):
        return pltpu.make_async_copy((m_in, v_in)[n].at[:, cols(k)], (m_stage, v_stage)[n].at[k % 2], state.at[k % 2, n])

    def state_out(k, n):
        return pltpu.make_async_copy((m_new, v_new)[n].at[k % 2], (m_out, v_out)[n].at[:, cols(k)], new_sem.at[k % 2, n])

    def grads(k):
        @pl.when(k >= 3)
        def _():
            for n in range(6):
                z_copy(k - 3, n).wait_send()

        s = k % 3
        g_send[s, 1] = product(k, 2).astype(bf)
        z_copy(k, 0).start()
        z_copy(k, 1).start()
        g_send[s, 0] = product(k, 1).astype(bf)
        z_copy(k, 2).start()
        g_send[s, 2] = product(k, 3).astype(bf)
        z_copy(k, 3).start()

    def relay(k):
        s = k % 3
        z_copy(k, 0).wait_recv()
        g_send[s, 0, lo] = (g_send[s, 0, lo].astype(f32) + r1[k, 0].astype(f32)).astype(bf)
        z_copy(k, 4).start()
        z_copy(k, 1).wait_recv()
        g_send[s, 2, hi] = (g_send[s, 2, hi].astype(f32) + r1[k, 1].astype(f32)).astype(bf)
        z_copy(k, 5).start()

    def gather_z(k):
        own = product(k, 0)
        for n in (2, 3, 4, 5):
            z_copy(k, n).wait_recv()
        raw_sum = own + r2[k, 0].astype(f32) + r2[k, 1].astype(f32)

        @pl.when(k >= 2)
        def _():
            h_copy(k - 2).wait_send()

        mine_first = h == 0
        x_send[k % 2] = jnp.where(mine_first, raw_sum[eighth:], raw_sum[:eighth]).astype(bf)
        h_copy(k).start()
        pick[k % 2] = jnp.where(mine_first, raw_sum[:eighth], raw_sum[eighth:])
        for n in range(2):
            state_in(k, n).start()

    def adam(k):
        h_copy(k).wait_recv()
        g = pick[k % 2] + x_recv[k].astype(f32)
        for n in range(2):
            state_in(k, n).wait()

        @pl.when(k >= 2)
        def _():
            for n in range(2):
                m_copy(k - 2, n).wait_send()
                state_out(k - 2, n).wait()

        s = k % 2
        m1 = beta_one * m_stage[s] + (1.0 - beta_one) * g
        v1 = beta_two * v_stage[s] + (1.0 - beta_two) * g * g
        m_new[s] = m1
        v_new[s] = v1
        m_send[s] = m1.astype(bf)
        v_send[s] = v1.astype(bf)
        for n in range(2):
            m_copy(k, n).start()
            state_out(k, n).start()

    def wide(j):
        return pl.ds(pl.multiple_of(j * dw, dw), dw)

    def w_copy(j):
        rows = pl.ds(pl.multiple_of(j * dw, dw), dw)
        return pltpu.make_async_copy(w.at[rows, pl.ds(0, hid2)], w_stage, load.at[4])

    def s_copy(j):
        return remote(s_send.at[j % 2], s_recv.at[j], ss_sem.at[j % 2], sr_sem.at[j], sib)

    def l_copy(j):
        return remote(l_send.at[j % 2], l_recv.at[j], ls_sem.at[j % 2], lr_sem.at[j], across)

    def y_copy(j, n):
        b = j % 2
        src = (l_own.at[j, 2, pl.ds(0, 64)], l_own.at[j, 2, pl.ds(64, 64)], y_send.at[b, 0], y_send.at[b, 1])[n]
        dst = (y1.at[j, 0], y1.at[j, 1], y2.at[j, 0], y2.at[j, 1])[n]
        return remote(src, dst, ys_sem.at[b, n], yr_sem.at[j, n], up_y if n % 2 == 0 else down_y)

    def t_copy(j):
        return pltpu.make_async_copy(t_out.at[j % 2], tok_grad.at[:, wide(j)], t_sem.at[j % 2])

    def inputs_back(j):
        w_copy(j).wait()

        @pl.when(j >= 2)
        def _():
            s_copy(j - 2).wait_send()

        b = j % 2
        dx = (
            lax.dot_general(
                ha[:, pl.ds(0, hid2)], w_stage[...], (((1,), (1,)), ((), ())), preferred_element_type=f32
            )
            * scale_w
        ).astype(bf)
        for r in range(8):
            at = ORDER.index(r) * pair
            back = lax.dot_general(
                onehot[r], dx[at : at + pair], (((0,), (0,)), ((), ())), preferred_element_type=f32
            ).astype(bf)
            s_own[b, r] = back[:128]
            s_send[b, r] = back[128:]
        s_copy(j).start()

        @pl.when(j + 1 < n_col)
        def _():
            w_copy(j + 1).start()

    def add_core(j):
        b = j % 2
        s_copy(j).wait_recv()

        @pl.when(j >= 2)
        def _():
            l_copy(j - 2).wait_send()

        for dy in range(4):
            l_send[b, dy] = (s_own[b, 2 * dy + 1].astype(f32) + s_recv[j, 2 * dy + 1].astype(f32)).astype(bf)
        l_copy(j).start()
        for dy in range(4):
            l_own[j, dy] = (s_own[b, 2 * dy].astype(f32) + s_recv[j, 2 * dy].astype(f32)).astype(bf)

    def add_across(j):
        l_copy(j).wait_recv()
        for dy in (2, 1, 3, 0):
            l_own[j, dy] = (l_own[j, dy].astype(f32) + l_recv[j, dy].astype(f32)).astype(bf)
        y_copy(j, 0).start()
        y_copy(j, 1).start()

    def add_relay(j):
        b = j % 2
        top, low = pl.ds(0, 64), pl.ds(64, 64)
        y_copy(j, 0).wait_recv()
        y_copy(j, 1).wait_recv()

        @pl.when(j >= 2)
        def _():
            for n in range(4):
                y_copy(j - 2, n).wait_send()

        y_send[b, 0, top] = (l_own[j, 1, top].astype(f32) + y1[j, 0].astype(f32)).astype(bf)
        y_send[b, 0, low] = l_own[j, 1, low]
        y_send[b, 1, top] = l_own[j, 3, top]
        y_send[b, 1, low] = (l_own[j, 3, low].astype(f32) + y1[j, 1].astype(f32)).astype(bf)
        y_copy(j, 2).start()
        y_copy(j, 3).start()

    def add_last(j):
        @pl.when(j >= 2)
        def _():
            t_copy(j - 2).wait()

        b = j % 2

        y_copy(j, 2).wait_recv()
        y_copy(j, 3).wait_recv()
        t_out[b] = (l_own[j, 0].astype(f32) + y2[j, 0].astype(f32) + y2[j, 1].astype(f32)).astype(bf)
        t_copy(j).start()

    w_copy(0).start()

    def stage(t, delay, count, body):
        k = t - delay

        @pl.when((k >= 0) & (k < count))
        def _():
            body(k)

    @pl.loop(0, n_chunk + 4)
    def _(t):
        stage(t, 0, n_chunk, grads)

        @pl.when(t == 0)
        def _():
            far_w.start()

        stage(t, 4, n_chunk, adam)
        stage(t, 0, n_col, inputs_back)
        stage(t, 1, n_chunk, relay)
        stage(t, 1, n_col, add_core)
        stage(t, 2, n_col, add_across)
        stage(t, 3, n_col, add_relay)
        stage(t, 3, n_chunk, gather_z)
        stage(t, 4, n_col, add_last)

    for k in range(n_chunk - 3, n_chunk):
        for n in range(6):
            z_copy(k, n).wait_send()
    for k in range(n_chunk - 2, n_chunk):
        h_copy(k).wait_send()
        for n in range(2):
            m_copy(k, n).wait_send()
            state_out(k, n).wait()
    for j in range(n_col - 2, n_col):
        s_copy(j).wait_send()
        l_copy(j).wait_send()
        for n in range(4):
            y_copy(j, n).wait_send()
        t_copy(j).wait()
    far_w.wait()
    for k in range(n_chunk):
        for n in range(2):
            m_copy(k, n).wait_recv()


def reduce(x, cots, ha, onehot, weights, moment_one, moment_two, scales):
    width, total = weights.shape
    rows = moment_one.shape[0]
    bf, f32 = jnp.bfloat16, jnp.float32
    sems = pltpu.SemaphoreType.DMA
    small = jax.ShapeDtypeStruct((rows, total), bf)
    large = jax.ShapeDtypeStruct((rows, total), f32)
    return pl.pallas_call(
        functools.partial(reduce_kernel, scales),
        name="reduce",
        out_shape=(jax.ShapeDtypeStruct((128, width), bf), large, large, small, small, small),
        in_specs=[ANY] * 7,
        out_specs=(ANY,) * 6,
        scratch_shapes=[
            pltpu.VMEM((2, 4, 640, 896), bf),
            pltpu.VMEM((896, 2304), bf),
            pltpu.VMEM((8, 112, 256), bf),
            pltpu.VMEM((2, 896, 640), bf),
            pltpu.VMEM((3, 3, 640, 256), bf),
            pltpu.VMEM((9, 2, 320, 256), bf),
            pltpu.VMEM((9, 2, 640, 256), bf),
            pltpu.VMEM((2, 320, 256), bf),
            pltpu.VMEM((9, 320, 256), bf),
            pltpu.VMEM((2, 320, 256), f32),
            pltpu.VMEM((2, 320, 256), f32),
            pltpu.VMEM((2, 320, 256), f32),
            pltpu.VMEM((2, 320, 256), f32),
            pltpu.VMEM((2, 320, 256), bf),
            pltpu.VMEM((2, 320, 256), bf),
            pltpu.VMEM((512, 1536), bf),
            pltpu.VMEM((2, 320, 256), f32),
            pltpu.VMEM((2, 8, 128, 512), bf),
            pltpu.VMEM((2, 8, 128, 512), bf),
            pltpu.VMEM((5, 8, 128, 512), bf),
            pltpu.VMEM((5, 4, 128, 512), bf),
            pltpu.VMEM((5, 4, 128, 512), bf),
            pltpu.VMEM((2, 4, 128, 512), bf),
            pltpu.VMEM((5, 2, 64, 512), bf),
            pltpu.VMEM((5, 2, 128, 512), bf),
            pltpu.VMEM((2, 2, 128, 512), bf),
            pltpu.VMEM((2, 128, 512), bf),
            sems(()),
            sems(()),
            sems((5,)),
            sems((3, 6)),
            sems((9, 2)),
            sems((9, 4)),
            sems((2,)),
            sems((9,)),
            sems((2, 2)),
            sems((2, 2)),
            sems((2, 2)),
            sems((9, 2)),
            sems((2,)),
            sems((5,)),
            sems((2,)),
            sems((5,)),
            sems((2, 4)),
            sems((5, 4)),
            sems((2,)),
        ],
        compiler_params=pltpu.CompilerParams(
            collective_id=2, has_side_effects=True, vmem_limit_bytes=60 * 2**20
        ),
    )(x, cots, ha, onehot, weights, moment_one, moment_two)


def place_kernel(info, w, w_got, m_own, v_own, m_got, v_got, w_new, m_new, v_new):
    def write(rows, first, second):
        weight = rows.astype(jnp.float32)
        first_hat = first * (1.0 / (1.0 - beta_one**adam_step))
        second_hat = second * (1.0 / (1.0 - beta_two**adam_step))
        m_new[0] = first
        v_new[0] = second
        w_new[0] = (
            weight - learn_rate * (first_hat / (jnp.sqrt(second_hat) + adam_eps) + decay_rate * weight)
        ).astype(w_new.dtype)

    @pl.when(info[0] == 0)
    def _():
        write(w[...], m_own[...], v_own[...])

    @pl.when(info[0] != 0)
    def _():
        write(w_got[...], m_got[...].astype(jnp.float32), v_got[...].astype(jnp.float32))


def place(info, weights, w_got, m_own, v_own, m_got, v_got):
    rows, total = m_own.shape
    step = 64
    steps = rows // step
    stay = pl.BlockSpec((step, total), lambda i, f: (jnp.where(f[0] == 0, i, 0), 0))
    move = pl.BlockSpec((step, total), lambda i, f: (jnp.where(f[0] == 0, 0, i), 0))
    old = pl.BlockSpec((step, total), lambda i, f: (f[1] * steps + jnp.where(f[0] == 0, i, 0), 0))
    out = pl.BlockSpec((1, step, total), lambda i, f: (0, i, 0))
    return pl.pallas_call(
        place_kernel,
        name="place",
        grid_spec=pltpu.PrefetchScalarGridSpec(
            num_scalar_prefetch=1,
            grid=(steps,),
            in_specs=[old, move, stay, stay, move, move],
            out_specs=(out, out, out),
        ),
        out_shape=(
            jax.ShapeDtypeStruct((1, rows, total), jnp.bfloat16),
            jax.ShapeDtypeStruct((1, rows, total), jnp.float32),
            jax.ShapeDtypeStruct((1, rows, total), jnp.float32),
        ),
        compiler_params=pltpu.CompilerParams(vmem_limit_bytes=40 * 2**20),
    )(info, weights, w_got, m_own, v_own, m_got, v_got)


def shards(tokens, expert_ids, gate_q, cotangent, placement, weights, moment_one, moment_two):
    my_slot = lax.axis_index("expert")
    dp_index = lax.axis_index("dp")
    width = tokens.shape[1]
    hidden = weights.shape[2] // 3
    scales = (width ** (-0.5), hidden ** (-0.5))
    pack = jnp.concatenate(
        [
            jnp.pad(expert_ids.T, ((0, 2), (0, 0)), constant_values=-1),
            jnp.pad(gate_q.T, ((0, 2), (0, 0))),
        ],
        axis=0,
    )
    x, cots, ha, onehot, _ = dispatch(tokens, cotangent, pack, weights[0], scales)
    token_grad, m_own, v_own, w_got, m_got, v_got = reduce(
        x, cots, ha, onehot, weights[0], moment_one[0], moment_two[0], scales
    )
    moving = (placement[my_slot] != my_slot).astype(jnp.int32)
    info = jnp.stack([moving, dp_index.astype(jnp.int32)])
    new_w, new_m, new_v = place(info, weights[0], w_got, m_own, v_own, m_got, v_got)
    return (token_grad, new_w, new_m, new_v)


def solution(mesh):
    placed = (
        P(("dp", "expert"), None),
        P(("dp", "expert"), None),
        P(("dp", "expert"), None),
        P(("dp", "expert"), None),
        P(),
        P("expert", None, None),
        P("expert", "dp", None),
        P("expert", "dp", None),
    )
    return jax.shard_map(
        shards,
        mesh=mesh,
        in_specs=placed,
        out_specs=(
            P(("dp", "expert"), None),
            P("expert", "dp", None),
            P("expert", "dp", None),
            P("expert", "dp", None),
        ),
        check_vma=False,
    )
```

time: 530 us -> 265 us (0.50); the launches traced: 523 us -> 263 us
  waiting for transfers between devices: 268 us -> 0 us
  Pallas kernels: 0 us -> 251 us
  local copies, waits for them, and re-layouts: 108 us -> 9.22 us
  matrix products: 56.3 us -> 0 us
  other arithmetic: 51.7 us -> 1.38 us
  starting transfers between devices: 22.9 us -> 0 us
  between operations: 15.2 us -> 1.33 us
    pallas_call x0 -> x3, Pallas kernels: none -> 251 us  [the longest x1 145 us: reduce(): pl.pallas_call(functools.partial(reduce_kernel, scales), name='reduce', o...]
    unnamed x2 -> x0, waiting for transfers between devices: 140 us -> none
    all_to_all x3 -> x0, waiting for transfers between devices: 87.8 us -> none  [the longest x1 40.4 us: shards(): lax.all_to_all(send_cots, 'expert', split_axis=0, concat_axis=0, tiled=True)]
    dot_general x5 -> x0, matrix products: 56.3 us -> none  [the longest x1 13.7 us: shards(): jnp.dot(recv_inputs, in_cols, preferred_element_type=jnp.float32)]
    ppermute x3 -> x0, waiting for transfers between devices: 40.8 us -> none  [partner(): return lax.ppermute(value, axis, pairs)]
    unnamed x27 -> x15, local copies, waits for them, and re-layouts: 45.7 us -> 8.63 us
    gather x4 -> x0, local copies, waits for them, and re-layouts: 29.1 us -> none  [the longest x2 18.5 us: shards(): returned[slots].astype(jnp.float32).reshape(tok_rows, top_k, model_width)]
    broadcast_in_dim x3 -> x0, other arithmetic: 16.6 us -> none  [shards(): return (token_grad, new_rows[None], new_one[None], new_two[None])]
  transfers between devices with their start and end apart: 7 -> 0, of which waited for: 7 -> 0; matrix products, arithmetic and copies ran while one was open for 23% -> 0% of each run, Pallas kernels for 0% -> 0%
where the time goes in v1:
time: 265 us; the launch traced here: 263 us
  Pallas kernels  251 us (95%)
  local copies, waits for them, and re-layouts  9.22 us (3%)
    pallas_call x1, Pallas kernels, reduce(): pl.pallas_call(functools.partial(reduce_kernel, scales), name='reduce', o...  145 us
    pallas_call x1, Pallas kernels, dispatch(): pl.pallas_call(functools.partial(dispatch_kernel, scales), name='dispatch...  100 us
    unnamed x15, local copies, waits for them, and re-layouts  8.63 us
    pallas_call x1, Pallas kernels, place(): pl.pallas_call(place_kernel, name='place', grid_spec=pltpu.PrefetchScalar...  6.17 us

profile of v1, /device:TPU:0, one launch (start us, length us, event | category | flops | bytes accessed | tf_op | source)
XLA Modules:
  0.0 263.2 jit_solution(13181599762534620365)
XLA Ops:
  0.6 1.3 pad_add_fusion.pack
  1.9 100.1 %dispatch.1 = (bf16[896,2560]{1,0:T(8,128)(2,1)}, bf16[896,2560]{1,0:T(8,128)(2,1)}, bf16[896,2304]{1,0:T(8,128)(2,1)}, bf16[8,112,256]{2,1,0:T(8,128)(2,1)}, bf16[2,8,256,2560]{3,2,1,0:T(8,128)(2,1)}) custom-call(bf16[128,2560]{1,0:T(8,128)(2,1)} %tok.1, bf16[128,2560]{1,0:T(8,128)(2,1)} %cot.1, s32[16,128]{1,0:T(8,128)} %pad_add_fusion.pack, ...), custom_call_target="tpu_custom_call" | custom-call | tf_op jit(solution)/shard_map/dispatch/pallas_call | solution.py:319
  102.1 0.0 copy-start.6
  102.1 145.0 %reduce.1 = (bf16[128,2560]{1,0:T(8,128)(2,1)}, f32[320,2304]{1,0:T(8,128)}, f32[320,2304]{1,0:T(8,128)}, bf16[320,2304]{1,0:T(8,128)(2,1)}, bf16[320,2304]{1,0:T(8,128)(2,1)}, /*index=5*/bf16[320,2304]{1,0:T(8,128)(2,1)}) custom-call(bf16[896,2560]{1,0:T(8,128)(2,1)} %get-tuple-element.17.x_in, bf16[896,2560]{1,0:T(8,128)(2,1)} %get-tuple-element.18.c_in, ...), custom_call_target="tpu_custom_call" | custom-call | tf_op jit(solution)/shard_map/reduce/pallas_call | solution.py:750
  247.1 0.0 copy-done.6
  247.1 0.6 dynamic_slice.3
  248.3 0.1 pad_add_fusion.1.info
  248.4 0.0 copy-start
  248.4 1.8 copy-done
  250.2 0.0 copy-start.1
  250.2 1.8 copy-done.1
  252.1 0.0 copy-start.2
  252.1 1.4 copy-done.2
  253.4 0.0 copy-start.3
  253.4 1.4 copy-done.3
  254.8 0.0 copy-start.4
  254.8 1.4 copy-done.4
  256.2 0.0 copy-start.5
  256.2 6.2 %place.1 = (bf16[1,320,2304]{2,1,0:T(8,128)(2,1)}, f32[1,320,2304]{2,1,0:T(8,128)}, f32[1,320,2304]{2,1,0:T(8,128)}) custom-call(s32[2]{0:T(128)S(1)} %pad_add_fusion.1.info, bf16[2560,2304]{1,0:T(8,128)(2,1)} %bitcast.10, bf16[320,2304]{1,0:T(8,128)(2,1)S(1)} %copy-done.2, f32[320,2304]{1,0:T(8,128)S(1)} %copy-done, f32[320,2304]{1,0:T(8,128)S(1)} %copy-done.1, ...), custom_call_target="tpu_custom_call" | custom-call | tf_op jit(solution)/shard_map/place/pallas_call | solution.py:838
  262.4 0.0 copy-done.5
  262.4 0.8 copy.13
Async XLA Ops:
  102.1 145.0 %copy-start.6 = (s32[16]{0:T(128)S(1)}, s32[16]{0:T(128)}, u32[]{:S(2)}) copy-start(s32[16]{0:T(128)} %param.12) | copy-start | bytes 196
  248.4 1.8 copy-start
  250.2 1.8 copy-start.1
  252.1 1.4 copy-start.2
  253.4 1.4 copy-start.3
  254.8 1.4 copy-start.4
  256.2 6.2 %copy-start.5 = (bf16[128,2560]{1,0:T(8,128)(2,1)S(1)}, bf16[128,2560]{1,0:T(8,128)(2,1)}, u32[]{:S(2)}) copy-start(bf16[128,2560]{1,0:T(8,128)(2,1)} %get-tuple-element.34) | copy-start | bytes 1966084

commit v2 on v1

v2 whole, which is shorter than its diff:
```python
import functools

import jax
import jax.numpy as jnp
from jax import lax
from jax.experimental import pallas as pl
from jax.experimental.pallas import tpu as pltpu
from jax.sharding import PartitionSpec as P

beta_one = 0.9
beta_two = 0.95
learn_rate = 0.02
decay_rate = 0.1
adam_eps = 1e-08
adam_step = 20.0

MESH = pl.DeviceIdType.MESH
ANY = pl.BlockSpec(memory_space=pl.ANY)
VMEM = pl.BlockSpec(memory_space=pltpu.VMEM)

ORDER = (0, 1, 2, 3, 6, 7, 4, 5)
BATCHES = ((0, 1), (2, 3, 6, 7), (4, 5))


def coords():
    dp = lax.axis_index("dp")
    e = lax.axis_index("expert")
    return dp, e, e // 4, (e // 2) % 2, e % 2


def peer(dy, dl, dc):
    dp, _, y, l, c = coords()
    y2 = (y + dy) % 4 if dy else y
    l2 = 1 - l if dl else l
    c2 = 1 - c if dc else c
    return (dp, y2 * 4 + l2 * 2 + c2)


def dispatch_kernel(
    scales,
    tok,
    cot,
    pack,
    w,
    xt_out,
    ha_out,
    p_out,
    gathered,
    ids,
    mrow,
    grow,
    gcol,
    onehot,
    wv,
    stage,
    xc,
    xt,
    pre,
    ha,
    psend,
    precv,
    send,
    recv,
    local,
    outs,
):
    scale_w, scale_h = scales
    _, me, _, _, _ = coords()
    cap, pair = 56, 128
    hid = pre.shape[1] // 2
    chips = [(dy, dl, 0) for dy in range(4) for dl in range(2)][1:]
    others = chips + [(0, 0, 1)]

    barrier = pltpu.get_barrier_semaphore()
    for o in others:
        pl.semaphore_signal(barrier, inc=1, device_id=peer(*o), device_id_type=MESH)
    pl.semaphore_wait(barrier, len(others))

    packs = []
    for n, (dy, dl, dc) in enumerate(chips):
        packs.append(
            pltpu.make_async_remote_copy(
                src_ref=pack,
                dst_ref=ids.at[0, ((4 - dy) % 4) * 2 + dl],
                send_sem=psend.at[n],
                recv_sem=precv.at[n],
                device_id=peer(dy, dl, dc),
                device_id_type=MESH,
            )
        )
    for d in packs:
        d.start()
    ids[0, 0] = pack[...]

    flight = {}

    def go(i, key, src, r, rows, to):
        n = len(flight)
        d = pltpu.make_async_remote_copy(
            src_ref=src,
            dst_ref=gathered.at[i, r, pl.ds(128 * to[2] + rows[0], rows[1] - rows[0])],
            send_sem=send.at[n],
            recv_sem=recv.at[n],
            device_id=peer(*to),
            device_id_type=MESH,
        )
        d.start()
        flight[(i, key)] = d

    UP, DOWN, ACROSS, SIB = (1, 0, 0), (3, 0, 0), (0, 1, 0), (0, 0, 1)
    own = (tok, cot)

    def mine(i, lo, hi):
        return own[i].at[pl.ds(lo, hi - lo)]

    def got(i, r, lo, hi):
        return gathered.at[i, r, pl.ds(lo, hi - lo)]

    def share(i, r, lo, hi):
        go(i, ("S", r, lo), got(i, r, lo, hi), r, (lo, hi), SIB)

    def land(i, key):
        flight[(i, key)].wait_recv()

    cut = (80, 64)
    fork = ((48, 32), (32, 32))
    fork_b = (96, 96)

    def first(i):
        a = cut[i]
        go(i, "A1", mine(i, 0, a), 1, (0, a), ACROSS)
        go(i, "B1p", mine(i, a, 128), 6, (a, 128), UP)
        go(i, "B1m", mine(i, a, 128), 2, (a, 128), DOWN)
        go(i, "A2p0", mine(i, 0, a), 6, (0, a), UP)
        go(i, "A2m0", mine(i, 0, a), 2, (0, a), DOWN)
        go(i, "B30", mine(i, a, 128), 1, (a, 128), ACROSS)
        go(i, ("S", 0, 0), own[i], 0, (0, 128), SIB)

    def second(i):
        a, f = cut[i], fork[i][0]
        land(i, "A1")
        go(i, "A2p1", got(i, 1, 0, a), 7, (0, a), UP)
        go(i, "A2m1", got(i, 1, 0, a), 3, (0, a), DOWN)
        share(i, 1, 0, a)
        land(i, "A2p0")
        go(i, "A3p0", got(i, 6, 0, f), 4, (0, f), UP)
        share(i, 6, 0, a)
        land(i, "A2m0")
        go(i, "A3m0", got(i, 2, f, a), 4, (f, a), DOWN)
        share(i, 2, 0, a)

    def third(i):
        a, b = cut[i], fork_b[i]
        land(i, "B1p")
        go(i, "B33", got(i, 6, a, 128), 7, (a, 128), ACROSS)
        go(i, "B2p", got(i, 6, a, b), 4, (a, b), UP)
        share(i, 6, a, 128)
        land(i, "B1m")
        go(i, "B31", got(i, 2, a, 128), 3, (a, 128), ACROSS)
        go(i, "B2m", got(i, 2, b, 128), 4, (b, 128), DOWN)
        share(i, 2, a, 128)
        land(i, "B30")
        share(i, 1, a, 128)

    def fourth(i):
        a, f = cut[i], fork[i][1]
        land(i, "A2p1")
        go(i, "A3p1", got(i, 7, 0, f), 5, (0, f), UP)
        share(i, 7, 0, a)
        land(i, "A2m1")
        go(i, "A3m1", got(i, 3, f, a), 5, (f, a), DOWN)
        share(i, 3, 0, a)
        land(i, "B2p")
        land(i, "B2m")
        go(i, "B32", got(i, 4, a, 128), 5, (a, 128), ACROSS)
        land(i, "A3p0")
        land(i, "A3m0")
        share(i, 4, 0, a)
        share(i, 4, a, 128)
        land(i, "B33")
        share(i, 7, a, 128)
        land(i, "B31")
        share(i, 3, a, 128)

    def fifth(i):
        a = cut[i]
        land(i, "A3p1")
        land(i, "A3m1")
        share(i, 5, 0, a)
        land(i, "B32")
        share(i, 5, a, 128)

    def fetch(i, batch):
        copies = []
        for n, r in enumerate(batch):
            if r == 0:
                land(i, ("S", 0, 0))
                copies.append(pltpu.make_async_copy(own[i], stage.at[n, pl.ds(0, 128)], local.at[n]))
                copies.append(
                    pltpu.make_async_copy(
                        gathered.at[i, 0, pl.ds(128, 128)], stage.at[n, pl.ds(128, 128)], local.at[4]
                    )
                )
            else:
                land(i, ("S", r, 0))
                land(i, ("S", r, cut[i]))
                copies.append(pltpu.make_async_copy(gathered.at[i, r], stage.at[n], local.at[n]))
        for d in copies:
            d.start()
        for d in copies:
            d.wait()

    def pick(i, batch):
        fetch(i, batch)
        for n, r in enumerate(batch):
            at = ORDER.index(r) * pair
            rows = jnp.dot(onehot[r], stage[n], preferred_element_type=jnp.float32)
            if i == 1:
                rows = rows * gcol[pl.ds(at, pair), :]
            rows = rows.astype(jnp.bfloat16)
            xc[pl.ds(n * pair, pair), :] = rows
            for col in range(0, rows.shape[1], 128):
                xt[i, pl.ds(col, 128), pl.ds(at, pair)] = rows[:, col : col + 128].T
        at, size = span(batch)
        out(xt.at[i, :, pl.ds(at, size)], xt_out.at[i, :, pl.ds(at, size)])

    def out(src, dst):
        d = pltpu.make_async_copy(src, dst, outs.at[len(written)])
        d.start()
        written.append(d)

    written = []

    def span(batch):
        return ORDER.index(batch[0]) * pair, len(batch) * pair

    def forward(batch):
        at, size = span(batch)
        wide = 512

        @pl.loop(0, 2 * hid // wide)
        def _(n):
            cols = pl.ds(pl.multiple_of(n * wide, wide), wide)
            pre[pl.ds(at, size), cols] = (
                jnp.dot(xc[pl.ds(0, size), :], wv[:, cols], preferred_element_type=jnp.float32)
                * scale_w
            )

    def backward(batch):
        at, size = span(batch)
        wide = 256

        @pl.loop(0, hid // wide)
        def _(n):
            def cols(start):
                return pl.ds(pl.multiple_of(start + n * wide, wide), wide)

            rows = pl.ds(at, size)
            da = (
                jnp.dot(xc[pl.ds(0, size), :], wv[:, cols(2 * hid)], preferred_element_type=jnp.float32)
                * scale_h
            )
            gate = pre[rows, cols(0)]
            up = pre[rows, cols(hid)]
            sig = jax.nn.sigmoid(gate)
            gs = gate * sig
            ha[rows, cols(0)] = (da * up * sig * (1.0 + gate * (1.0 - sig))).astype(jnp.bfloat16)
            ha[rows, cols(hid)] = (da * gs).astype(jnp.bfloat16)
            ha[rows, cols(2 * hid)] = (gs * up).astype(jnp.bfloat16)

        out(ha.at[pl.ds(at, size)], ha_out.at[pl.ds(at, size)])

    first(0)
    weights_in = pltpu.make_async_copy(w, wv, local.at[5])
    weights_in.start()
    for d in packs:
        d.wait_recv()
    swap = pltpu.make_async_remote_copy(
        src_ref=ids.at[0],
        dst_ref=ids.at[1],
        send_sem=psend.at[7],
        recv_sem=precv.at[7],
        device_id=peer(*SIB),
        device_id_type=MESH,
    )
    swap.start()
    second(0)
    swap.wait_recv()
    for r in range(8):
        for core in range(2):
            s = 2 * r + core
            chosen = ids[core, r, 0:8, :] == me
            mrow[s : s + 1, :] = jnp.sum(jnp.where(chosen, 1.0, 0.0), axis=0, keepdims=True)
            grow[s : s + 1, :] = jnp.sum(
                jnp.where(chosen, ids[core, r, 8:16, :].astype(jnp.float32), 0.0), axis=0, keepdims=True
            ) * (1.0 / 65536.0)
    before = (
        lax.broadcasted_iota(jnp.int32, (128, 128), 0) < lax.broadcasted_iota(jnp.int32, (128, 128), 1)
    ).astype(jnp.bfloat16)
    position = jnp.dot(mrow[...].astype(jnp.bfloat16), before, preferred_element_type=jnp.float32)
    mrow[...] = jnp.where(mrow[...] > 0.5, position, -1000.0)
    slot = lax.broadcasted_iota(jnp.int32, (pair, 256), 0).astype(jnp.float32)
    for r in range(8):
        place = jnp.concatenate([mrow[2 * r : 2 * r + 1, :], mrow[2 * r + 1 : 2 * r + 2, :] + cap], axis=1)
        gate_row = jnp.concatenate([grow[2 * r : 2 * r + 1, :], grow[2 * r + 1 : 2 * r + 2, :]], axis=1)
        hit = jnp.where(slot == place, 1.0, 0.0)
        onehot[r] = hit.astype(jnp.bfloat16)
        gcol[pl.ds(ORDER.index(r) * pair, pair), :] = jnp.sum(hit * gate_row, axis=1, keepdims=True)
    out(onehot, p_out)
    third(0)
    first(1)
    pick(0, BATCHES[0])
    weights_in.wait()
    forward(BATCHES[0])
    fourth(0)
    second(1)
    pick(0, BATCHES[1])
    forward(BATCHES[1])
    fifth(0)
    third(1)
    pick(0, BATCHES[2])
    forward(BATCHES[2])
    pick(1, BATCHES[0])
    backward(BATCHES[0])
    fourth(1)
    pick(1, BATCHES[1])
    backward(BATCHES[1])
    fifth(1)
    pick(1, BATCHES[2])
    backward(BATCHES[2])
    for d in packs:
        d.wait_send()
    swap.wait_send()
    for d in flight.values():
        d.wait_send()
    for d in written:
        d.wait()


def dispatch(tokens, cotangent, pack, weights, scales):
    width = tokens.shape[1]
    total = weights.shape[1]
    hid = total // 3
    slots = 1024
    bf, f32 = jnp.bfloat16, jnp.float32
    sems = pltpu.SemaphoreType.DMA
    return pl.pallas_call(
        functools.partial(dispatch_kernel, scales),
        name="dispatch",
        out_shape=(
            jax.ShapeDtypeStruct((2, width, slots), bf),
            jax.ShapeDtypeStruct((slots, total), bf),
            jax.ShapeDtypeStruct((8, 128, 256), bf),
            jax.ShapeDtypeStruct((2, 8, 256, width), bf),
        ),
        in_specs=[ANY, ANY, VMEM, ANY],
        out_specs=(ANY,) * 4,
        scratch_shapes=[
            pltpu.VMEM((2, 8, 16, 128), jnp.int32),
            pltpu.VMEM((16, 128), f32),
            pltpu.VMEM((16, 128), f32),
            pltpu.VMEM((slots, 1), f32),
            pltpu.VMEM((8, 128, 256), bf),
            pltpu.VMEM((width, total), bf),
            pltpu.VMEM((4, 256, width), bf),
            pltpu.VMEM((512, width), bf),
            pltpu.VMEM((2, width, slots), bf),
            pltpu.VMEM((slots, 2 * hid), f32),
            pltpu.VMEM((slots, total), bf),
            sems((8,)),
            sems((8,)),
            sems((64,)),
            sems((64,)),
            sems((6,)),
            sems((10,)),
        ],
        compiler_params=pltpu.CompilerParams(
            collective_id=1, has_side_effects=True, vmem_limit_bytes=60 * 2**20
        ),
    )(tokens, cotangent, pack, weights)


def reduce_kernel(
    scales,
    xt_in,
    ha_in,
    p_in,
    w,
    m_in,
    v_in,
    tok_grad,
    m_out,
    v_out,
    w_got,
    m_got,
    v_got,
    xt,
    ha,
    onehot,
    g_send,
    r1,
    r2,
    x_send,
    x_recv,
    m_stage,
    v_stage,
    m_new,
    v_new,
    m_send,
    v_send,
    w_stage,
    pick,
    s_send,
    s_own,
    s_recv,
    l_recv,
    l_own,
    l_send,
    y1,
    y2,
    y_send,
    t_out,
    far_send,
    far_recv,
    load,
    z_send,
    r1_sem,
    r2_sem,
    xs_sem,
    xr_sem,
    state,
    new_sem,
    ms_sem,
    mr_sem,
    ss_sem,
    sr_sem,
    ls_sem,
    lr_sem,
    ys_sem,
    yr_sem,
    t_sem,
):
    scale_w, scale_h = scales
    dp, e, y, l, c = coords()
    z, h = dp // 2, dp % 2
    bf, f32 = jnp.bfloat16, jnp.float32
    up_z = (((z + 1) % 4) * 2 + h, e)
    down_z = (((z + 3) % 4) * 2 + h, e)
    other_h = (z * 2 + 1 - h, e)
    far = peer(2, 0, 0)
    sib = peer(0, 0, 1)
    across = peer(0, 1, 0)
    up_y = peer(1, 0, 0)
    down_y = peer(3, 0, 0)

    n_chunk, n_col = 9, 10
    cw = 256
    dw = 256
    quarter, eighth = 640, 320
    hid2 = 1536
    pair = 128

    barrier = pltpu.get_barrier_semaphore()
    greet = [up_z, down_z, other_h, far, sib, across, up_y, down_y]
    for d in greet:
        pl.semaphore_signal(barrier, inc=1, device_id=d, device_id_type=MESH)

    def rows_in(i, q):
        start = pl.multiple_of(((z + q) % 4) * quarter, quarter)
        return pltpu.make_async_copy(xt_in.at[i, pl.ds(start, quarter)], xt.at[i, q], load.at[4 * i + q])

    rows_in(0, 2).start()
    ha_load = pltpu.make_async_copy(ha_in, ha, load.at[8])
    ha_load.start()
    for q in (1, 3, 0):
        rows_in(0, q).start()
    onehot_load = pltpu.make_async_copy(p_in, onehot, load.at[9])
    onehot_load.start()
    for q in (2, 1, 3, 0):
        rows_in(1, q).start()
    pl.semaphore_wait(barrier, len(greet))

    def remote(src, dst, ssem, rsem, to):
        return pltpu.make_async_remote_copy(
            src_ref=src, dst_ref=dst, send_sem=ssem, recv_sem=rsem, device_id=to, device_id_type=MESH
        )

    own_rows = pl.ds(pl.multiple_of(dp * eighth, eighth), eighth)
    far_w = remote(w.at[own_rows], w_got, far_send, far_recv, far)

    def cols(k):
        return pl.ds(pl.multiple_of(k * cw, cw), cw)

    def product(k, q):
        scale = jnp.where(k < 6, scale_w, scale_h).astype(f32)
        return (
            jnp.dot(xt[k // 6, q], ha[:, cols(k)], preferred_element_type=f32) * scale
        )

    lo, hi = pl.ds(0, eighth), pl.ds(eighth, eighth)

    def z_copy(k, n):
        s = k % 3
        src = (
            g_send.at[s, 1, lo],
            g_send.at[s, 1, hi],
            g_send.at[s, 0, hi],
            g_send.at[s, 2, lo],
            g_send.at[s, 0, lo],
            g_send.at[s, 2, hi],
        )[n]
        dst = (
            r1.at[k, 0],
            r1.at[k, 1],
            r2.at[k, 0, hi],
            r2.at[k, 1, lo],
            r2.at[k, 0, lo],
            r2.at[k, 1, hi],
        )[n]
        rsem = (r1_sem.at[k, 0], r1_sem.at[k, 1], r2_sem.at[k, 0], r2_sem.at[k, 1], r2_sem.at[k, 2], r2_sem.at[k, 3])[n]
        return remote(src, dst, z_send.at[s, n], rsem, up_z if n % 2 == 0 else down_z)

    def h_copy(k):
        return remote(x_send.at[k % 3], x_recv.at[k], xs_sem.at[k % 3], xr_sem.at[k], other_h)

    def m_copy(k, n):
        src = (m_send, v_send)[n].at[k]
        dst = (m_got, v_got)[n].at[:, cols(k)]
        return remote(src, dst, ms_sem.at[k, n], mr_sem.at[k, n], far)

    def state_in(k, n):
        return pltpu.make_async_copy((m_in, v_in)[n].at[:, cols(k)], (m_stage, v_stage)[n].at[k % 3], state.at[k % 3, n])

    def state_out(k, n):
        return pltpu.make_async_copy((m_new, v_new)[n].at[k % 2], (m_out, v_out)[n].at[:, cols(k)], new_sem.at[k % 2, n])

    def grads(k):
        @pl.when(k >= 3)
        def _():
            for n in range(6):
                z_copy(k - 3, n).wait_send()

        s = k % 3

        @pl.when(k == 0)
        def _():
            rows_in(0, 2).wait()
            ha_load.wait()

        @pl.when(k == 6)
        def _():
            for q in range(4):
                rows_in(1, q).wait()

        g_send[s, 1] = product(k, 2).astype(bf)
        z_copy(k, 0).start()
        z_copy(k, 1).start()

        @pl.when(k == 0)
        def _():
            for q in (1, 3, 0):
                rows_in(0, q).wait()

        g_send[s, 0] = product(k, 1).astype(bf)
        z_copy(k, 2).start()
        g_send[s, 2] = product(k, 3).astype(bf)
        z_copy(k, 3).start()

    def relay(k):
        s = k % 3
        z_copy(k, 0).wait_recv()
        g_send[s, 0, lo] = (g_send[s, 0, lo].astype(f32) + r1[k, 0].astype(f32)).astype(bf)
        z_copy(k, 4).start()
        z_copy(k, 1).wait_recv()
        g_send[s, 2, hi] = (g_send[s, 2, hi].astype(f32) + r1[k, 1].astype(f32)).astype(bf)
        z_copy(k, 5).start()

    def gather_z(k):
        own = product(k, 0)
        for n in (2, 3, 4, 5):
            z_copy(k, n).wait_recv()
        raw_sum = own + r2[k, 0].astype(f32) + r2[k, 1].astype(f32)

        @pl.when(k >= 3)
        def _():
            h_copy(k - 3).wait_send()

        mine_first = h == 0
        x_send[k % 3] = jnp.where(mine_first, raw_sum[eighth:], raw_sum[:eighth]).astype(bf)
        h_copy(k).start()
        pick[k % 3] = jnp.where(mine_first, raw_sum[:eighth], raw_sum[eighth:])
        for n in range(2):
            state_in(k, n).start()

    def adam(k):
        h_copy(k).wait_recv()
        g = pick[k % 3] + x_recv[k].astype(f32)
        for n in range(2):
            state_in(k, n).wait()

        @pl.when(k >= 2)
        def _():
            for n in range(2):
                state_out(k - 2, n).wait()

        s = k % 2
        m1 = beta_one * m_stage[k % 3] + (1.0 - beta_one) * g
        v1 = beta_two * v_stage[k % 3] + (1.0 - beta_two) * g * g
        m_new[s] = m1
        v_new[s] = v1
        m_send[k] = m1.astype(bf)
        v_send[k] = v1.astype(bf)
        for n in range(2):
            m_copy(k, n).start()
            state_out(k, n).start()

    def wide(j):
        return pl.ds(pl.multiple_of(j * dw, dw), dw)

    def w_copy(j):
        rows = pl.ds(pl.multiple_of(j * dw, dw), dw)
        return pltpu.make_async_copy(w.at[rows, pl.ds(0, hid2)], w_stage.at[j % 2], load.at[10 + j % 2])

    def s_copy(j):
        return remote(s_send.at[j % 2], s_recv.at[j], ss_sem.at[j % 2], sr_sem.at[j], sib)

    def l_copy(j):
        return remote(l_send.at[j % 4], l_recv.at[j], ls_sem.at[j % 4], lr_sem.at[j], across)

    def y_copy(j, n):
        src = (l_own.at[j, 2, pl.ds(0, 64)], l_own.at[j, 2, pl.ds(64, 64)], y_send.at[j, 0], y_send.at[j, 1])[n]
        dst = (y1.at[j, 0], y1.at[j, 1], y2.at[j, 0], y2.at[j, 1])[n]
        return remote(src, dst, ys_sem.at[j, n], yr_sem.at[j, n], up_y if n % 2 == 0 else down_y)

    def t_copy(j):
        return pltpu.make_async_copy(t_out.at[j % 2], tok_grad.at[:, wide(j)], t_sem.at[j % 2])

    def inputs_back(j):
        w_copy(j).wait()

        @pl.when(j >= 2)
        def _():
            s_copy(j - 2).wait_send()

        b = j % 2
        dx = (
            lax.dot_general(
                ha[:, pl.ds(0, hid2)], w_stage[j % 2], (((1,), (1,)), ((), ())), preferred_element_type=f32
            )
            * scale_w
        ).astype(bf)
        for r in range(8):
            at = ORDER.index(r) * pair
            back = lax.dot_general(
                onehot[r], dx[at : at + pair], (((0,), (0,)), ((), ())), preferred_element_type=f32
            ).astype(bf)
            s_own[b, r] = back[:128]
            s_send[b, r] = back[128:]
        s_copy(j).start()

        @pl.when(j + 2 < n_col)
        def _():
            w_copy(j + 2).start()

    def add_core(j):
        b = j % 2
        s_copy(j).wait_recv()

        @pl.when(j >= 4)
        def _():
            l_copy(j - 4).wait_send()

        for dy in range(4):
            l_send[j % 4, dy] = (s_own[b, 2 * dy + 1].astype(f32) + s_recv[j, 2 * dy + 1].astype(f32)).astype(bf)
        l_copy(j).start()
        for dy in range(4):
            l_own[j, dy] = (s_own[b, 2 * dy].astype(f32) + s_recv[j, 2 * dy].astype(f32)).astype(bf)

    def add_across(j):
        l_copy(j).wait_recv()
        for dy in (2, 1, 3, 0):
            l_own[j, dy] = (l_own[j, dy].astype(f32) + l_recv[j, dy].astype(f32)).astype(bf)
        y_copy(j, 0).start()
        y_copy(j, 1).start()

    def add_relay(j):
        top, low = pl.ds(0, 64), pl.ds(64, 64)
        y_copy(j, 0).wait_recv()
        y_copy(j, 1).wait_recv()

        y_send[j, 0, top] = (l_own[j, 1, top].astype(f32) + y1[j, 0].astype(f32)).astype(bf)
        y_send[j, 0, low] = l_own[j, 1, low]
        y_send[j, 1, top] = l_own[j, 3, top]
        y_send[j, 1, low] = (l_own[j, 3, low].astype(f32) + y1[j, 1].astype(f32)).astype(bf)
        y_copy(j, 2).start()
        y_copy(j, 3).start()

    def add_last(j):
        @pl.when(j >= 2)
        def _():
            t_copy(j - 2).wait()

        b = j % 2

        y_copy(j, 2).wait_recv()
        y_copy(j, 3).wait_recv()
        t_out[b] = (l_own[j, 0].astype(f32) + y2[j, 0].astype(f32) + y2[j, 1].astype(f32)).astype(bf)
        t_copy(j).start()

    w_copy(0).start()
    w_copy(1).start()

    def twice(body):
        def both(i):
            body(2 * i)
            body(2 * i + 1)

        return both

    def stage(t, delay, count, body):
        k = t - delay

        @pl.when((k >= 0) & (k < count))
        def _():
            body(k)

    @pl.loop(0, n_chunk + 3)
    def _(t):
        stage(t, 0, n_chunk, grads)

        @pl.when(t == 0)
        def _():
            onehot_load.wait()
            far_w.start()

        stage(t, 1, n_col // 2, twice(add_core))
        stage(t, 0, n_col // 2, twice(inputs_back))
        stage(t, 0, n_chunk, relay)
        stage(t, 1, n_chunk, gather_z)
        stage(t, 2, n_chunk, adam)
        stage(t, 3, n_col // 2, twice(add_across))
        stage(t, 4, n_col // 2, twice(add_relay))
        stage(t, 6, n_col // 2, twice(add_last))

    for k in range(n_chunk - 3, n_chunk):
        for n in range(6):
            z_copy(k, n).wait_send()
    for k in range(n_chunk - 3, n_chunk):
        h_copy(k).wait_send()
    for k in range(n_chunk - 2, n_chunk):
        for n in range(2):
            state_out(k, n).wait()
    for j in range(n_col - 2, n_col):
        s_copy(j).wait_send()
        t_copy(j).wait()
    for j in range(n_col - 4, n_col):
        l_copy(j).wait_send()
    for j in range(n_col):
        for n in range(4):
            y_copy(j, n).wait_send()
    far_w.wait()
    for k in range(n_chunk):
        for n in range(2):
            m_copy(k, n).wait()


def reduce(xt, ha, onehot, weights, moment_one, moment_two, scales):
    width, total = weights.shape
    rows = moment_one.shape[0]
    bf, f32 = jnp.bfloat16, jnp.float32
    sems = pltpu.SemaphoreType.DMA
    small = jax.ShapeDtypeStruct((rows, total), bf)
    large = jax.ShapeDtypeStruct((rows, total), f32)
    return pl.pallas_call(
        functools.partial(reduce_kernel, scales),
        name="reduce",
        out_shape=(jax.ShapeDtypeStruct((128, width), bf), large, large, small, small, small),
        in_specs=[ANY] * 6,
        out_specs=(ANY,) * 6,
        scratch_shapes=[
            pltpu.VMEM((2, 4, 640, 1024), bf),
            pltpu.VMEM((1024, 2304), bf),
            pltpu.VMEM((8, 128, 256), bf),
            pltpu.VMEM((3, 3, 640, 256), bf),
            pltpu.VMEM((9, 2, 320, 256), bf),
            pltpu.VMEM((9, 2, 640, 256), bf),
            pltpu.VMEM((3, 320, 256), bf),
            pltpu.VMEM((9, 320, 256), bf),
            pltpu.VMEM((3, 320, 256), f32),
            pltpu.VMEM((3, 320, 256), f32),
            pltpu.VMEM((2, 320, 256), f32),
            pltpu.VMEM((2, 320, 256), f32),
            pltpu.VMEM((9, 320, 256), bf),
            pltpu.VMEM((9, 320, 256), bf),
            pltpu.VMEM((2, 256, 1536), bf),
            pltpu.VMEM((3, 320, 256), f32),
            pltpu.VMEM((2, 8, 128, 256), bf),
            pltpu.VMEM((2, 8, 128, 256), bf),
            pltpu.VMEM((10, 8, 128, 256), bf),
            pltpu.VMEM((10, 4, 128, 256), bf),
            pltpu.VMEM((10, 4, 128, 256), bf),
            pltpu.VMEM((4, 4, 128, 256), bf),
            pltpu.VMEM((10, 2, 64, 256), bf),
            pltpu.VMEM((10, 2, 128, 256), bf),
            pltpu.VMEM((10, 2, 128, 256), bf),
            pltpu.VMEM((2, 128, 256), bf),
            sems(()),
            sems(()),
            sems((12,)),
            sems((3, 6)),
            sems((9, 2)),
            sems((9, 4)),
            sems((3,)),
            sems((9,)),
            sems((3, 2)),
            sems((2, 2)),
            sems((9, 2)),
            sems((9, 2)),
            sems((2,)),
            sems((10,)),
            sems((4,)),
            sems((10,)),
            sems((10, 4)),
            sems((10, 4)),
            sems((2,)),
        ],
        compiler_params=pltpu.CompilerParams(
            collective_id=2, has_side_effects=True, vmem_limit_bytes=60 * 2**20
        ),
    )(xt, ha, onehot, weights, moment_one, moment_two)


def place_kernel(info, w, w_got, m_own, v_own, m_got, v_got, w_new, m_new, v_new):
    def write(rows, first, second):
        weight = rows.astype(jnp.float32)
        first_hat = first * (1.0 / (1.0 - beta_one**adam_step))
        second_hat = second * (1.0 / (1.0 - beta_two**adam_step))
        m_new[0] = first
        v_new[0] = second
        w_new[0] = (
            weight - learn_rate * (first_hat / (jnp.sqrt(second_hat) + adam_eps) + decay_rate * weight)
        ).astype(w_new.dtype)

    @pl.when(info[0] == 0)
    def _():
        write(w[...], m_own[...], v_own[...])

    @pl.when(info[0] != 0)
    def _():
        write(w_got[...], m_got[...].astype(jnp.float32), v_got[...].astype(jnp.float32))


def place(info, weights, w_got, m_own, v_own, m_got, v_got):
    rows, total = m_own.shape
    step = 160
    steps = rows // step
    stay = pl.BlockSpec((step, total), lambda i, f: (jnp.where(f[0] == 0, i, 0), 0))
    move = pl.BlockSpec((step, total), lambda i, f: (jnp.where(f[0] == 0, 0, i), 0))
    old = pl.BlockSpec((step, total), lambda i, f: (f[1] * steps + jnp.where(f[0] == 0, i, 0), 0))
    out = pl.BlockSpec((1, step, total), lambda i, f: (0, i, 0))
    return pl.pallas_call(
        place_kernel,
        name="place",
        grid_spec=pltpu.PrefetchScalarGridSpec(
            num_scalar_prefetch=1,
            grid=(steps,),
            in_specs=[old, move, stay, stay, move, move],
            out_specs=(out, out, out),
        ),
        out_shape=(
            jax.ShapeDtypeStruct((1, rows, total), jnp.bfloat16),
            jax.ShapeDtypeStruct((1, rows, total), jnp.float32),
            jax.ShapeDtypeStruct((1, rows, total), jnp.float32),
        ),
        compiler_params=pltpu.CompilerParams(vmem_limit_bytes=60 * 2**20),
    )(info, weights, w_got, m_own, v_own, m_got, v_got)


def shards(tokens, expert_ids, gate_q, cotangent, placement, weights, moment_one, moment_two):
    my_slot = lax.axis_index("expert")
    dp_index = lax.axis_index("dp")
    width = tokens.shape[1]
    hidden = weights.shape[2] // 3
    scales = (width ** (-0.5), hidden ** (-0.5))
    pack = jnp.concatenate(
        [
            jnp.pad(expert_ids.T, ((0, 2), (0, 0)), constant_values=-1),
            jnp.pad(gate_q.T, ((0, 2), (0, 0))),
        ],
        axis=0,
    )
    xt, ha, onehot, _ = dispatch(tokens, cotangent, pack, weights[0], scales)
    token_grad, m_own, v_own, w_got, m_got, v_got = reduce(
        xt, ha, onehot, weights[0], moment_one[0], moment_two[0], scales
    )
    moving = (placement[my_slot] != my_slot).astype(jnp.int32)
    info = jnp.stack([moving, dp_index.astype(jnp.int32)])
    new_w, new_m, new_v = place(info, weights[0], w_got, m_own, v_own, m_got, v_got)
    return (token_grad, new_w, new_m, new_v)


def solution(mesh):
    placed = (
        P(("dp", "expert"), None),
        P(("dp", "expert"), None),
        P(("dp", "expert"), None),
        P(("dp", "expert"), None),
        P(),
        P("expert", None, None),
        P("expert", "dp", None),
        P("expert", "dp", None),
    )
    return jax.shard_map(
        shards,
        mesh=mesh,
        in_specs=placed,
        out_specs=(
            P(("dp", "expert"), None),
            P("expert", "dp", None),
            P("expert", "dp", None),
            P("expert", "dp", None),
        ),
        check_vma=False,
    )
```

time: 265 us -> 244 us (0.921)
  Pallas kernels: 251 us -> 238 us
  local copies, waits for them, and re-layouts: 9.22 us -> 1.44 us
    pallas_call x1, Pallas kernels: 100 us -> 92.3 us  [dispatch(): pl.pallas_call(functools.partial(dispatch_kernel, scales), name='dispatch...]
    unnamed x15 -> x5, local copies, waits for them, and re-layouts: 8.63 us -> 0.85 us
    pallas_call x1, Pallas kernels: 145 us -> 138 us  [reduce(): pl.pallas_call(functools.partial(reduce_kernel, scales), name='reduce', o...]
where the time goes in v2:
time: 244 us; the launch traced here: 243 us
  Pallas kernels  238 us (98%)
    pallas_call x1, Pallas kernels, reduce(): pl.pallas_call(functools.partial(reduce_kernel, scales), name='reduce', o...  138 us
    pallas_call x1, Pallas kernels, dispatch(): pl.pallas_call(functools.partial(dispatch_kernel, scales), name='dispatch...  92.3 us
    pallas_call x1, Pallas kernels, place(): pl.pallas_call(place_kernel, name='place', grid_spec=pltpu.PrefetchScalar...  7.76 us

profile of v2, /device:TPU:0, one launch (start us, length us, event | category | flops | bytes accessed | tf_op | source)
XLA Modules:
  0.0 242.8 jit_solution(7535516260777664547)
XLA Ops:
  0.6 1.3 pad_add_fusion.pack
  1.9 92.3 %dispatch.1 = (bf16[2,2560,1024]{2,1,0:T(8,128)(2,1)}, bf16[1024,2304]{1,0:T(8,128)(2,1)}, bf16[8,128,256]{2,1,0:T(8,128)(2,1)}, bf16[2,8,256,2560]{3,2,1,0:T(8,128)(2,1)}) custom-call(bf16[128,2560]{1,0:T(8,128)(2,1)} %tok.1, bf16[128,2560]{1,0:T(8,128)(2,1)} %cot.1, s32[16,128]{1,0:T(8,128)} %pad_add_fusion.pack, bf16[2560,2304]{1,0:T(8,128)(2,1)} %bitcast.8), custom_call_target="tpu_custom_call" | custom-call | tf_op jit(solution)/shard_map/dispatch/pallas_call | solution.py:347
  94.2 0.0 copy-start.1
  94.2 138.1 %reduce.1 = (bf16[128,2560]{1,0:T(8,128)(2,1)}, f32[320,2304]{1,0:T(8,128)}, f32[320,2304]{1,0:T(8,128)}, bf16[320,2304]{1,0:T(8,128)(2,1)}, bf16[320,2304]{1,0:T(8,128)(2,1)}, /*index=5*/bf16[320,2304]{1,0:T(8,128)(2,1)}) custom-call(bf16[2,2560,1024]{2,1,0:T(8,128)(2,1)} %get-tuple-element.16.xt_in, bf16[1024,2304]{1,0:T(8,128)(2,1)} %get-tuple-element.17.ha_in, ...), custom_call_target="tpu_custom_call" | custom-call | tf_op jit(solution)/shard_map/reduce/pallas_call | solution.py:774
  232.4 0.0 copy-done.1
  232.4 0.6 dynamic_slice.3
  233.6 0.6 pad_add_fusion.1.info
  234.2 0.0 copy-start
  234.2 7.8 %place.1 = (bf16[1,320,2304]{2,1,0:T(8,128)(2,1)}, f32[1,320,2304]{2,1,0:T(8,128)}, f32[1,320,2304]{2,1,0:T(8,128)}) custom-call(s32[2]{0:T(128)} %pad_add_fusion.1.info, bf16[2560,2304]{1,0:T(8,128)(2,1)} %bitcast.10, bf16[320,2304]{1,0:T(8,128)(2,1)} %get-tuple-element.20.w_got, f32[320,2304]{1,0:T(8,128)} %get-tuple-element.21.m_own, ...), custom_call_target="tpu_custom_call" | custom-call | tf_op jit(solution)/shard_map/place/pallas_call | solution.py:861
  242.0 0.0 copy-done
  242.0 0.8 copy.13
Async XLA Ops:
  94.2 138.1 %copy-start.1 = (s32[16]{0:T(128)S(1)}, s32[16]{0:T(128)}, u32[]{:S(2)}) copy-start(s32[16]{0:T(128)} %param.12) | copy-start | bytes 196
  234.2 7.8 %copy-start = (bf16[128,2560]{1,0:T(8,128)(2,1)S(1)}, bf16[128,2560]{1,0:T(8,128)(2,1)}, u32[]{:S(2)}) copy-start(bf16[128,2560]{1,0:T(8,128)(2,1)} %get-tuple-element.32) | copy-start | bytes 1966084

commit v3 on v2

--- a/solution.py
+++ b/solution.py
@@ -525,7 +525,7 @@
 
     def m_copy(k, n):
         src = (m_send, v_send)[n].at[k]
-        dst = (m_got, v_got)[n].at[:, cols(k)]
+        dst = (m_got, v_got)[n].at[k]
         return remote(src, dst, ms_sem.at[k, n], mr_sem.at[k, n], far)
 
     def state_in(k, n):
@@ -736,11 +736,11 @@
         stage(t, 1, n_col // 2, twice(add_core))
         stage(t, 0, n_col // 2, twice(inputs_back))
         stage(t, 0, n_chunk, relay)
+        stage(t, 2, n_col // 2, twice(add_across))
+        stage(t, 3, n_col // 2, twice(add_relay))
         stage(t, 1, n_chunk, gather_z)
         stage(t, 2, n_chunk, adam)
-        stage(t, 3, n_col // 2, twice(add_across))
-        stage(t, 4, n_col // 2, twice(add_relay))
-        stage(t, 6, n_col // 2, twice(add_last))
+        stage(t, 5, n_col // 2, twice(add_last))
 
     for k in range(n_chunk - 3, n_chunk):
         for n in range(6):
@@ -771,10 +771,11 @@
     sems = pltpu.SemaphoreType.DMA
     small = jax.ShapeDtypeStruct((rows, total), bf)
     large = jax.ShapeDtypeStruct((rows, total), f32)
+    chunked = jax.ShapeDtypeStruct((total // 256, rows, 256), bf)
     return pl.pallas_call(
         functools.partial(reduce_kernel, scales),
         name="reduce",
-        out_shape=(jax.ShapeDtypeStruct((128, width), bf), large, large, small, small, small),
+        out_shape=(jax.ShapeDtypeStruct((128, width), bf), large, large, small, chunked, chunked),
         in_specs=[ANY] * 6,
         out_specs=(ANY,) * 6,
         scratch_shapes=[
@@ -831,32 +832,47 @@
 
 
 def place_kernel(info, w, w_got, m_own, v_own, m_got, v_got, w_new, m_new, v_new):
-    def write(rows, first, second):
+    def write(cols, rows, first, second):
         weight = rows.astype(jnp.float32)
         first_hat = first * (1.0 / (1.0 - beta_one**adam_step))
         second_hat = second * (1.0 / (1.0 - beta_two**adam_step))
-        m_new[0] = first
-        v_new[0] = second
-        w_new[0] = (
+        m_new[0, :, cols] = first
+        v_new[0, :, cols] = second
+        w_new[0, :, cols] = (
             weight - learn_rate * (first_hat / (jnp.sqrt(second_hat) + adam_eps) + decay_rate * weight)
         ).astype(w_new.dtype)
 
-    @pl.when(info[0] == 0)
+    chunks, _, cw = m_got.shape
+    stays = info[lax.axis_index("expert")] == lax.axis_index("expert")
+
+    @pl.when(stays)
     def _():
-        write(w[...], m_own[...], v_own[...])
-
-    @pl.when(info[0] != 0)
+        for k in range(chunks):
+            cols = slice(k * cw, (k + 1) * cw)
+            write(cols, w[:, cols], m_own[:, cols], v_own[:, cols])
+
+    @pl.when(jnp.logical_not(stays))
     def _():
-        write(w_got[...], m_got[...].astype(jnp.float32), v_got[...].astype(jnp.float32))
+        for k in range(chunks):
+            cols = slice(k * cw, (k + 1) * cw)
+            write(cols, w_got[:, cols], m_got[k].astype(jnp.float32), v_got[k].astype(jnp.float32))
 
 
 def place(info, weights, w_got, m_own, v_own, m_got, v_got):
     rows, total = m_own.shape
     step = 160
     steps = rows // step
-    stay = pl.BlockSpec((step, total), lambda i, f: (jnp.where(f[0] == 0, i, 0), 0))
-    move = pl.BlockSpec((step, total), lambda i, f: (jnp.where(f[0] == 0, 0, i), 0))
-    old = pl.BlockSpec((step, total), lambda i, f: (f[1] * steps + jnp.where(f[0] == 0, i, 0), 0))
+
+    def here(i, f):
+        return jnp.where(f[lax.axis_index("expert")] == lax.axis_index("expert"), i, 0)
+
+    def there(i, f):
+        return i - here(i, f)
+
+    stay = pl.BlockSpec((step, total), lambda i, f: (here(i, f), 0))
+    move = pl.BlockSpec((step, total), lambda i, f: (there(i, f), 0))
+    parts = pl.BlockSpec((m_got.shape[0], step, m_got.shape[2]), lambda i, f: (0, there(i, f), 0))
+    old = pl.BlockSpec((step, total), lambda i, f: (lax.axis_index("dp") * steps + here(i, f), 0))
     out = pl.BlockSpec((1, step, total), lambda i, f: (0, i, 0))
     return pl.pallas_call(
         place_kernel,
@@ -864,7 +880,7 @@
         grid_spec=pltpu.PrefetchScalarGridSpec(
             num_scalar_prefetch=1,
             grid=(steps,),
-            in_specs=[old, move, stay, stay, move, move],
+            in_specs=[old, move, stay, stay, parts, parts],
             out_specs=(out, out, out),
         ),
         out_shape=(
@@ -877,8 +893,6 @@
 
 
 def shards(tokens, expert_ids, gate_q, cotangent, placement, weights, moment_one, moment_two):
-    my_slot = lax.axis_index("expert")
-    dp_index = lax.axis_index("dp")
     width = tokens.shape[1]
     hidden = weights.shape[2] // 3
     scales = (width ** (-0.5), hidden ** (-0.5))
@@ -893,9 +907,7 @@
     token_grad, m_own, v_own, w_got, m_got, v_got = reduce(
         xt, ha, onehot, weights[0], moment_one[0], moment_two[0], scales
     )
-    moving = (placement[my_slot] != my_slot).astype(jnp.int32)
-    info = jnp.stack([moving, dp_index.astype(jnp.int32)])
-    new_w, new_m, new_v = place(info, weights[0], w_got, m_own, v_own, m_got, v_got)
+    new_w, new_m, new_v = place(placement, weights[0], w_got, m_own, v_own, m_got, v_got)
     return (token_grad, new_w, new_m, new_v)
 
 

time: 244 us -> 242 us (level)
  no operation moved by 1% of the time
where the time goes in v3:
time: 242 us; the launch traced here: 241 us
  Pallas kernels  238 us (98%)
    pallas_call x1, Pallas kernels, reduce(): pl.pallas_call(functools.partial(reduce_kernel, scales), name='reduce', o...  138 us
    pallas_call x1, Pallas kernels, dispatch(): pl.pallas_call(functools.partial(dispatch_kernel, scales), name='dispatch...  92.3 us
    pallas_call x1, Pallas kernels, place(): pl.pallas_call(place_kernel, name='place', grid_spec=pltpu.PrefetchScalar...  7.58 us

profile of v3, /device:TPU:0, one launch (start us, length us, event | category | flops | bytes accessed | tf_op | source)
XLA Modules:
  0.0 240.9 jit_solution(16777680275746683374)
XLA Ops:
  0.6 1.3 pad_add_fusion.pack
  1.9 92.3 %dispatch.1 = (bf16[2,2560,1024]{2,1,0:T(8,128)(2,1)}, bf16[1024,2304]{1,0:T(8,128)(2,1)}, bf16[8,128,256]{2,1,0:T(8,128)(2,1)}, bf16[2,8,256,2560]{3,2,1,0:T(8,128)(2,1)}) custom-call(bf16[128,2560]{1,0:T(8,128)(2,1)} %tok.1, bf16[128,2560]{1,0:T(8,128)(2,1)} %cot.1, s32[16,128]{1,0:T(8,128)} %pad_add_fusion.pack, bf16[2560,2304]{1,0:T(8,128)(2,1)} %bitcast.5), custom_call_target="tpu_custom_call" | custom-call | tf_op jit(solution)/shard_map/dispatch/pallas_call | solution.py:347
  94.2 138.2 %reduce.1 = (bf16[128,2560]{1,0:T(8,128)(2,1)}, f32[320,2304]{1,0:T(8,128)}, f32[320,2304]{1,0:T(8,128)}, bf16[320,2304]{1,0:T(8,128)(2,1)}, bf16[9,320,256]{2,1,0:T(8,128)(2,1)}, /*index=5*/bf16[9,320,256]{2,1,0:T(8,128)(2,1)}) custom-call(bf16[2,2560,1024]{2,1,0:T(8,128)(2,1)} %get-tuple-element.16.xt_in, bf16[1024,2304]{1,0:T(8,128)(2,1)} %get-tuple-element.17.ha_in, ...), custom_call_target="tpu_custom_call" | custom-call | tf_op jit(solution)/shard_map/reduce/pallas_call | solution.py:775
  232.4 0.0 copy-start
  232.4 7.6 %place.1 = (bf16[1,320,2304]{2,1,0:T(8,128)(2,1)}, f32[1,320,2304]{2,1,0:T(8,128)}, f32[1,320,2304]{2,1,0:T(8,128)}) custom-call(s32[16]{0:T(128)} %info.1, bf16[2560,2304]{1,0:T(8,128)(2,1)} %bitcast.7, bf16[320,2304]{1,0:T(8,128)(2,1)} %get-tuple-element.20.w_got, f32[320,2304]{1,0:T(8,128)} %get-tuple-element.21.m_own, ...), custom_call_target="tpu_custom_call" | custom-call | tf_op jit(solution)/shard_map/place/pallas_call | solution.py:877
  240.0 0.0 copy-done
  240.0 0.8 copy.13
Async XLA Ops:
  232.4 7.6 %copy-start = (bf16[128,2560]{1,0:T(8,128)(2,1)S(1)}, bf16[128,2560]{1,0:T(8,128)(2,1)}, u32[]{:S(2)}) copy-start(bf16[128,2560]{1,0:T(8,128)(2,1)} %get-tuple-element.32) | copy-start | bytes 1966084
